TPU v7x, 512 devices: a whole 4x8x8 slice. The times are simulated.
512 devices in a mesh: wide: 64 (over y_lo, x, z), head: 8 (over y_hi, core).
Axes of the slice: x: 4, y: 8 (y_hi: 4, y_lo: 2; y = y_hi * 2 + y_lo), z: 8, core: 2. Of those that a mesh axis runs over, the one named last changes fastest.
Arguments:
- query: bfloat16 [4096, 16384], P('wide', 'head'), may hold values from -128 to 128
- key_new: bfloat16 [4096, 1024], P('wide', 'head'), may hold values from -7 to 7
- value_new: bfloat16 [4096, 1024], P('wide', 'head'), may hold values from -6 to 6
- key_cache: bfloat16 [1024, 128, 1024], P(('wide', 'head')), may hold values from -6 to 6
- value_cache: bfloat16 [1024, 128, 1024], P(('wide', 'head')), may hold values from -6 to 6
- page_table: int32 [64, 16], replicated, may hold values from 0 to 1023, as said below
- prefix_len: int32 [64], replicated, may hold values from 1 to 2048
Outputs:
- attended: bfloat16 [4096, 16384], P('wide', 'head')
Inputs may be any that keep to these rules, and one draw needn't show every extreme that they name: `page_table`: slot s lies in store group s // 16 along wide; every slot holds exactly one page of one request. Each page of a request lies in its own store group: no store group holds more than one page of any one request.
All inputs are finite; a program needn't handle non-finite values.
Results may differ from a plain program's by a relative error of at most 0.015.
Values may be sent and summed in bfloat16 or wider, within the bound.
No kernel may reach another device: no remote copies, remote signals or barrier semaphores. Data moves between devices by JAX's collectives and lax.ppermute only.
A program may use at most 64 MiB of HBM per device.

v0:
```python
import jax
import jax.numpy as jnp
from jax import lax
from jax.sharding import PartitionSpec as P

HD = 128


neg_fill = -1e30
pages_per_turn = 4


def fresh_state(query_rows, fresh_keys, fresh_values, group_size):
    scores = jnp.einsum(
        "hre,nhe->hrn", query_rows, fresh_keys, preferred_element_type=jnp.float32
    ) * HD ** (-0.5)
    row_token = jnp.arange(query_rows.shape[1]) // group_size
    visible = jnp.arange(fresh_keys.shape[0])[None, :] <= row_token[:, None]
    scores = jnp.where(visible[None], scores, neg_fill)
    highest = jnp.max(scores, axis=-1)
    weights = jnp.exp(scores - highest[..., None])
    weight_sum = jnp.sum(weights, axis=-1)
    numerator = jnp.einsum(
        "hrn,nhe->hre",
        weights.astype(jnp.bfloat16),
        fresh_values,
        preferred_element_type=jnp.float32,
    )
    return (numerator, highest, weight_sum)


def online_block(carry_state, query_rows, key_block, value_block, visible):
    numerator, highest, weight_sum = carry_state
    heads, rows_count = (query_rows.shape[0], query_rows.shape[1])
    scores = jnp.einsum("hre,pkhe->hrpk", query_rows, key_block, preferred_element_type=jnp.float32)
    scores = scores.reshape(heads, rows_count, -1) * HD ** (-0.5)
    scores = jnp.where(visible[None, None, :], scores, neg_fill)
    peak_new = jnp.maximum(highest, jnp.max(scores, axis=-1))
    factor = jnp.exp(highest - peak_new)
    weights = jnp.exp(scores - peak_new[..., None])
    weight_sum = weight_sum * factor + jnp.sum(weights, axis=-1)
    rounded = weights.astype(jnp.bfloat16).reshape(
        heads, rows_count, key_block.shape[0], key_block.shape[1]
    )
    added = jnp.einsum("hrpk,pkhe->hre", rounded, value_block, preferred_element_type=jnp.float32)
    return (numerator * factor[..., None] + added, peak_new, weight_sum)


def prefix_pass(carry_state, query_rows, recv_k, recv_v, page_ids, item_ids, page_count, length):
    page_len = recv_k.shape[1]
    padding = jnp.zeros((pages_per_turn,), jnp.int32)
    page_ids = jnp.concatenate([page_ids, padding])
    item_ids = jnp.concatenate([item_ids, padding])
    turn_count = (page_count + pages_per_turn - 1) // pages_per_turn

    def advance(block_index, state_now):
        start_page = block_index * pages_per_turn
        block_pages = lax.dynamic_slice_in_dim(page_ids, start_page, pages_per_turn)
        block_items = lax.dynamic_slice_in_dim(item_ids, start_page, pages_per_turn)
        active = start_page + jnp.arange(pages_per_turn) < page_count
        key_block = jnp.take(recv_k, block_items, axis=0)
        value_block = jnp.take(recv_v, block_items, axis=0)
        position = block_pages[:, None] * page_len + jnp.arange(page_len)[None, :]
        visible = (active[:, None] & (position < length)).reshape(-1)
        return online_block(state_now, query_rows, key_block, value_block, visible)

    return lax.fori_loop(0, turn_count, advance, carry_state)


def choose_slots(matched, rank, store_slot, slot_count):
    wanted = jnp.arange(slot_count, dtype=jnp.int32)
    chosen = matched[:, None, :] & (rank[:, None, :] == wanted[None, :, None])
    return jnp.sum(jnp.where(chosen, store_slot[:, None, :], 0), axis=2)


def body(query, key_new, value_new, key_cache, value_cache, page_table, prefix_len):
    wide_count = lax.axis_size("wide")
    new_tok = query.shape[0]
    kv_local = key_new.shape[1] // HD
    group_size = query.shape[1] // key_new.shape[1]
    max_pages = page_table.shape[1]
    stored = key_cache.shape[0]
    page_len = key_cache.shape[1]
    heads_total = key_cache.shape[2] // HD
    own_index = lax.axis_index("wide")
    shaped_k = key_cache.reshape(stored, page_len, heads_total, HD)
    shaped_v = value_cache.reshape(stored, page_len, heads_total, HD)
    head_k, head_v = (
        lax.all_to_all(shaped_k, "head", split_axis=2, concat_axis=0, tiled=True),
        lax.all_to_all(shaped_v, "head", split_axis=2, concat_axis=0, tiled=True),
    )
    query_rows = query.reshape(new_tok, kv_local, group_size, HD).transpose(1, 0, 2, 3)
    query_rows = query_rows.reshape(kv_local, new_tok * group_size, HD)
    fresh_keys = key_new.reshape(new_tok, kv_local, HD)
    fresh_values = value_new.reshape(new_tok, kv_local, HD)
    carry_state = fresh_state(query_rows, fresh_keys, fresh_values, group_size)
    column = jnp.arange(max_pages, dtype=jnp.int32)
    store_group = page_table // max_pages
    store_slot = page_table % max_pages
    same_group = store_group[:, :, None] == store_group[:, None, :]
    earlier = column[None, :] < column[:, None]
    rank_all = jnp.sum(same_group & earlier[None], axis=2)
    pages_live = (prefix_len + page_len - 1) // page_len
    capacity = (max_pages + wide_count - 1) // wide_count
    own_group = jnp.take(store_group, own_index, axis=0)
    own_length = jnp.take(prefix_len, own_index, axis=0)
    own_live = jnp.take(pages_live, own_index, axis=0)
    slots = choose_slots(store_group == own_index, rank_all, store_slot, capacity)
    send_k = jnp.take(head_k, slots.reshape(-1), axis=0).reshape(
        wide_count, capacity, page_len, kv_local, HD
    )
    send_v = jnp.take(head_v, slots.reshape(-1), axis=0).reshape(
        wide_count, capacity, page_len, kv_local, HD
    )
    recv_k, recv_v = (
        lax.all_to_all(send_k, "wide", split_axis=0, concat_axis=0, tiled=True),
        lax.all_to_all(send_v, "wide", split_axis=0, concat_axis=0, tiled=True),
    )
    recv_k = recv_k.reshape(wide_count * capacity, page_len, kv_local, HD)
    recv_v = recv_v.reshape(wide_count * capacity, page_len, kv_local, HD)
    item_ids = own_group * capacity + jnp.take(rank_all, own_index, axis=0)
    carry_state = prefix_pass(
        carry_state, query_rows, recv_k, recv_v, column, item_ids, own_live, own_length
    )
    numerator, highest, weight_sum = carry_state
    mixed = numerator / weight_sum[..., None]
    mixed = mixed.reshape(kv_local, new_tok, group_size, HD).transpose(1, 0, 2, 3)
    return mixed.reshape(new_tok, kv_local * group_size * HD).astype(jnp.bfloat16)


def solution(mesh):
    in_specs = (
        P("wide", "head"),
        P("wide", "head"),
        P("wide", "head"),
        P(("wide", "head"), None, None),
        P(("wide", "head"), None, None),
        P(),
        P(),
    )
    out_specs = P("wide", "head")
    return jax.shard_map(body, mesh=mesh, in_specs=in_specs, out_specs=out_specs, check_vma=False)
```

profile of v0, /device:TPU:24, one launch (start us, length us, event | category | flops | bytes accessed | tf_op | source)
XLA Modules:
  0.0 204.5 jit_solution(9098100990083735365)
XLA Ops:
  0.0 1.4 copy.33
  1.4 0.9 copy.34
  2.2 6.7 %all-to-all-start = ((bf16[2,128,8,128]{1,3,0,2:T(8,128)(2,1)}), bf16[2,128,8,128]{1,3,0,2:T(8,128)(2,1)S(1)}, u32[]{:S(2)}, u32[]{:S(2)}) async-start(bf16[2,128,8,128]{1,3,0,2:T(8,128)(2,1)} %copy.34), calls=%async_computation | async-start | bytes 1048576 | tf_op jit(solution)/shard_map/all_to_all | solution.py:89
  8.9 0.3 copy.37
  9.2 0.8 copy.38
  10.0 11.9 %all-to-all-done = bf16[2,128,8,128]{1,3,0,2:T(8,128)(2,1)S(1)} async-done(((bf16[2,128,8,128]{1,3,0,2:T(8,128)(2,1)}), bf16[2,128,8,128]{1,3,0,2:T(8,128)(2,1)S(1)}, u32[]{:S(2)}, u32[]{:S(2)}) %all-to-all-start) | async-done | bytes 524320 | tf_op jit(solution)/shard_map/all_to_all | solution.py:89
  21.9 8.8 %all-to-all-start.2 = ((bf16[2,128,8,128]{1,3,0,2:T(8,128)(2,1)}), bf16[2,128,8,128]{1,3,0,2:T(8,128)(2,1)S(1)}, u32[]{:S(2)}, u32[]{:S(2)}) async-start(bf16[2,128,8,128]{1,3,0,2:T(8,128)(2,1)} %copy.38), calls=%async_computation.2 | async-start | bytes 1048576 | tf_op jit(solution)/shard_map/all_to_all | solution.py:90
  30.7 0.1 convert_reduce_fusion
  30.9 0.3 copy.35
  31.2 1.0 gather_fusion.2
  32.1 12.8 %all-to-all-done.2 = bf16[2,128,8,128]{1,3,0,2:T(8,128)(2,1)S(1)} async-done(((bf16[2,128,8,128]{1,3,0,2:T(8,128)(2,1)}), bf16[2,128,8,128]{1,3,0,2:T(8,128)(2,1)S(1)}, u32[]{:S(2)}, u32[]{:S(2)}) %all-to-all-start.2) | async-done | bytes 524320 | tf_op jit(solution)/shard_map/all_to_all | solution.py:90
  45.0 0.3 copy.39
  45.2 2.1 %gather_fusion.3 = bf16[64,128,128]{2,1,0:T(8,128)(2,1)} fusion(bf16[16,128,128]{2,1,0:T(8,128)(2,1)S(1)} %bitcast.113, s32[1024]{0:T(1024)S(1)} %pad_clamp_fusion.1), kind=kCustom, calls=%fused_computation.2.clone | custom fusion | bytes 4194560 | tf_op jit(solution)/shard_map/jit(_take)/gather | solution.py:112
  47.4 3.4 %fusion.12 = (bf16[64,1,128,1,128]{4,2,3,1,0:T(8,128)(2,1)}, bf16[64,1,128,1,128]{4,2,3,1,0:T(8,128)(2,1)S(1)}) fusion(bf16[64,128,128]{2,1,0:T(8,128)(2,1)} %gather_fusion.3, pred[64]{0:T(512)(128)(4,1)S(1)} %compare_and_fusion.1, bf16[64,128,128]{2,1,0:T(8,128)(2,1)S(1)} %gather_fusion.2), kind=kLoop, calls=%fused_computation.30 | loop fusion | flops 2097152 | bytes 8388672 | tf_op jit(solution)/shard_map/reshape | solution.py:112
  50.8 68.8 %all_to_all.46 = bf16[64,1,128,1,128]{4,2,3,1,0:T(8,128)(2,1)} all-to-all(bf16[64,1,128,1,128]{4,2,3,1,0:T(8,128)(2,1)S(1)} %get-tuple-element.173), channel_id=1, replica_groups=mesh['wide'=64,'head'=8] {'wide'}, dimensions={0} | all-to-all | bytes 4194304 | tf_op jit(solution)/shard_map/all_to_all | solution.py:116
  119.6 5.4 %all-to-all-start.3 = ((bf16[64,1,128,1,128]{4,2,3,1,0:T(8,128)(2,1)}), bf16[64,1,128,1,128]{4,2,3,1,0:T(8,128)(2,1)}, u32[]{:S(2)}, u32[]{:S(2)}) async-start(bf16[64,1,128,1,128]{4,2,3,1,0:T(8,128)(2,1)} %get-tuple-element.172), calls=%async_computation.3 | async-start | bytes 4194304 | tf_op jit(solution)/shard_map/all_to_all | solution.py:117
  125.0 0.6 dynamic-slice.8
  126.3 0.7 dynamic-slice.9
  126.9 0.1 reshape.201
  127.0 0.1 reshape_transpose_reshape.4
  127.2 0.2 select_reduce_fusion
  128.1 0.2 fusion.26
  128.3 0.3 convolution_bitcast_fusion.1
  128.6 0.1 fusion.15
  128.6 49.4 %all-to-all-done.3 = bf16[64,1,128,1,128]{4,2,3,1,0:T(8,128)(2,1)} async-done(((bf16[64,1,128,1,128]{4,2,3,1,0:T(8,128)(2,1)}), bf16[64,1,128,1,128]{4,2,3,1,0:T(8,128)(2,1)}, u32[]{:S(2)}, u32[]{:S(2)}) %all-to-all-start.3) | async-done | bytes 2097184 | tf_op jit(solution)/shard_map/all_to_all | solution.py:117
  178.1 25.4 %while.18 = (s32[]{:T(128)}, f32[1,1024,128]{2,1,0:T(8,128)S(1)}, f32[1,1024]{1,0:T(1,128)S(1)}, f32[1,1024]{1,0:T(1,128)S(1)}, s32[]{:T(128)}, /*index=5*/s32[]...) while((s32[]{:T(128)}, f32[1,1024,128]{2,1,0:T(8,128)S(1)}, ...), condition=%wide.region_7.11_spmd, body=%wide.region_4.10_spmd.sunk | while | flops 273027648 | bytes 8718187 | solution.py:67
  178.1 0.1 compare_and_fusion.3
  178.1 2.2 %gather_fusion = bf16[4,128,128]{2,1,0:T(8,128)(2,1)S(1)} fusion(bf16[64,128,128]{2,1,0:T(8,128)(2,1)} %bitcast.103, s32[1024]{0:T(1024)S(1)} %pad_clamp_fusion.3), kind=kCustom, calls=%fused_computation.1.clone.clone.1 | custom fusion | bytes 262160 | tf_op jit(solution)/shard_map/while/body/jit(_take)/gather | solution.py:61
  180.3 0.1 bitcast_select_fusion.6
  180.4 0.1 dynamic-slice_multiply_fusion.2
  180.5 0.1 fusion.42
  180.6 0.5 fusion.43
  181.0 0.5 fusion.44
  181.6 2.2 %gather_fusion.1 = bf16[4,128,128]{2,1,0:T(8,128)(2,1)S(1)} fusion(bf16[64,128,128]{2,1,0:T(8,128)(2,1)} %bitcast.110, s32[1024]{0:T(1024)S(1)} %pad_clamp_fusion.3), kind=kCustom, calls=%fused_computation.3.clone.clone.1 | custom fusion | bytes 262160 | tf_op jit(solution)/shard_map/while/body/jit(_take)/gather | solution.py:62
  183.8 0.6 fusion.45
  184.4 0.1 compare_and_fusion.3
  184.5 2.2 %gather_fusion = bf16[4,128,128]{2,1,0:T(8,128)(2,1)S(1)} fusion(bf16[64,128,128]{2,1,0:T(8,128)(2,1)} %bitcast.103, s32[1024]{0:T(1024)S(1)} %pad_clamp_fusion.3), kind=kCustom, calls=%fused_computation.1.clone.clone.1 | custom fusion | bytes 262160 | tf_op jit(solution)/shard_map/while/body/jit(_take)/gather | solution.py:61
  186.7 0.1 bitcast_select_fusion.6
  186.8 0.1 dynamic-slice_multiply_fusion.2
  186.9 0.1 fusion.42
  186.9 0.4 fusion.43
  187.4 0.5 fusion.44
  188.0 2.2 %gather_fusion.1 = bf16[4,128,128]{2,1,0:T(8,128)(2,1)S(1)} fusion(bf16[64,128,128]{2,1,0:T(8,128)(2,1)} %bitcast.110, s32[1024]{0:T(1024)S(1)} %pad_clamp_fusion.3), kind=kCustom, calls=%fused_computation.3.clone.clone.1 | custom fusion | bytes 262160 | tf_op jit(solution)/shard_map/while/body/jit(_take)/gather | solution.py:62
  190.1 0.6 fusion.45
  190.8 0.1 compare_and_fusion.3
  190.9 2.2 %gather_fusion = bf16[4,128,128]{2,1,0:T(8,128)(2,1)S(1)} fusion(bf16[64,128,128]{2,1,0:T(8,128)(2,1)} %bitcast.103, s32[1024]{0:T(1024)S(1)} %pad_clamp_fusion.3), kind=kCustom, calls=%fused_computation.1.clone.clone.1 | custom fusion | bytes 262160 | tf_op jit(solution)/shard_map/while/body/jit(_take)/gather | solution.py:61
  193.1 0.1 bitcast_select_fusion.6
  193.1 0.1 dynamic-slice_multiply_fusion.2
  193.2 0.1 fusion.42
  193.3 0.4 fusion.43
  193.8 0.5 fusion.44
  194.3 2.2 %gather_fusion.1 = bf16[4,128,128]{2,1,0:T(8,128)(2,1)S(1)} fusion(bf16[64,128,128]{2,1,0:T(8,128)(2,1)} %bitcast.110, s32[1024]{0:T(1024)S(1)} %pad_clamp_fusion.3), kind=kCustom, calls=%fused_computation.3.clone.clone.1 | custom fusion | bytes 262160 | tf_op jit(solution)/shard_map/while/body/jit(_take)/gather | solution.py:62
  196.5 0.6 fusion.45
  197.2 0.1 compare_and_fusion.3
  197.2 2.2 %gather_fusion = bf16[4,128,128]{2,1,0:T(8,128)(2,1)S(1)} fusion(bf16[64,128,128]{2,1,0:T(8,128)(2,1)} %bitcast.103, s32[1024]{0:T(1024)S(1)} %pad_clamp_fusion.3), kind=kCustom, calls=%fused_computation.1.clone.clone.1 | custom fusion | bytes 262160 | tf_op jit(solution)/shard_map/while/body/jit(_take)/gather | solution.py:61
  199.4 0.1 bitcast_select_fusion.6
  199.5 0.1 dynamic-slice_multiply_fusion.2
  199.6 0.1 fusion.42
  199.7 0.4 fusion.43
  200.1 0.5 fusion.44
  200.7 2.2 %gather_fusion.1 = bf16[4,128,128]{2,1,0:T(8,128)(2,1)S(1)} fusion(bf16[64,128,128]{2,1,0:T(8,128)(2,1)} %bitcast.110, s32[1024]{0:T(1024)S(1)} %pad_clamp_fusion.3), kind=kCustom, calls=%fused_computation.3.clone.clone.1 | custom fusion | bytes 262160 | tf_op jit(solution)/shard_map/while/body/jit(_take)/gather | solution.py:62
  202.9 0.6 fusion.45
  203.5 0.2 divide_convert_fusion
  203.7 0.8 convert_element_type.20
  (40 shorter events, 0.3 us)
Async XLA Ops:
  0.0 128.3 %copy-start = (bf16[64,128]{1,0:T(8,128)(2,1)S(1)}, bf16[64,128]{1,0:T(8,128)(2,1)}, u32[]{:S(2)}) copy-start(bf16[64,128]{1,0:T(8,128)(2,1)} %param.17) | copy-start | bytes 49156
  0.0 8.9 %copy-start.2 = (bf16[2,128,1024]{2,1,0:T(8,128)(2,1)S(1)}, bf16[2,128,1024]{2,1,0:T(8,128)(2,1)}, u32[]{:S(2)}) copy-start(bf16[2,128,1024]{2,1,0:T(8,128)(2,1)} %param.19) | copy-start | bytes 1572868
  2.2 28.4 %copy-start.3 = (s32[64,16]{0,1:T(8,128)S(1)}, s32[64,16]{0,1:T(8,128)}, u32[]{:S(2)}) copy-start(s32[64,16]{0,1:T(8,128)} %param.20) | copy-start | bytes 12292
  2.2 19.7 %all-to-all-start = ((bf16[2,128,8,128]{1,3,0,2:T(8,128)(2,1)}), bf16[2,128,8,128]{1,3,0,2:T(8,128)(2,1)S(1)}, u32[]{:S(2)}, u32[]{:S(2)}) async-start(bf16[2,128,8,128]{1,3,0,2:T(8,128)(2,1)} %copy.34), calls=%async_computation | async-start | bytes 1048576 | tf_op jit(solution)/shard_map/all_to_all | solution.py:89
  21.9 23.0 %all-to-all-start.2 = ((bf16[2,128,8,128]{1,3,0,2:T(8,128)(2,1)}), bf16[2,128,8,128]{1,3,0,2:T(8,128)(2,1)S(1)}, u32[]{:S(2)}, u32[]{:S(2)}) async-start(bf16[2,128,8,128]{1,3,0,2:T(8,128)(2,1)} %copy.38), calls=%async_computation.2 | async-start | bytes 1048576 | tf_op jit(solution)/shard_map/all_to_all | solution.py:90
  119.5 5.4 %copy-start.5 = (s32[64]{0:T(128)S(1)}, s32[64]{0:T(128)}, u32[]{:S(2)}) copy-start(s32[64]{0:T(128)} %param.21) | copy-start | bytes 772
  119.5 7.4 %copy-start.1 = (bf16[64,2048]{1,0:T(8,128)(2,1)S(1)}, bf16[64,2048]{1,0:T(8,128)(2,1)}, u32[]{:S(2)}) copy-start(bf16[64,2048]{1,0:T(8,128)(2,1)} %param.15) | copy-start | bytes 786436
  119.6 8.5 %copy-start.4 = (bf16[64,128]{1,0:T(8,128)(2,1)S(1)}, bf16[64,128]{1,0:T(8,128)(2,1)}, u32[]{:S(2)}) copy-start(bf16[64,128]{1,0:T(8,128)(2,1)} %param.16) | copy-start | bytes 49156
  119.6 58.5 %all-to-all-start.3 = ((bf16[64,1,128,1,128]{4,2,3,1,0:T(8,128)(2,1)}), bf16[64,1,128,1,128]{4,2,3,1,0:T(8,128)(2,1)}, u32[]{:S(2)}, u32[]{:S(2)}) async-start(bf16[64,1,128,1,128]{4,2,3,1,0:T(8,128)(2,1)} %get-tuple-element.172), calls=%async_computation.3 | async-start | bytes 4194304 | tf_op jit(solution)/shard_map/all_to_all | solution.py:117
  125.0 53.1 %copy-start.6 = (s32[20]{0:T(128)S(1)}, s32[20]{0:T(128)}, u32[]{:S(2)}) copy-start(s32[20]{0:T(128)} %constant.152.clone.1) | copy-start | bytes 244
where the time goes:
time: 204 us; the launch traced here: 205 us
  waiting for transfers between devices  74.1 us (36%)
  blocking collectives  68.8 us (34%)
  local copies, waits for them, and re-layouts  26.6 us (13%)
  starting transfers between devices  20.8 us (10%)
  other arithmetic  7.58 us (4%)
  matrix products  4.73 us (2%)
    all_to_all x1, blocking collectives, body(): lax.all_to_all(send_k, 'wide', split_axis=0, concat_axis=0, tiled=True)  68.8 us
    all_to_all x1, waiting for transfers between devices, body(): lax.all_to_all(send_v, 'wide', split_axis=0, concat_axis=0, tiled=True)  49.4 us
    all_to_all x1, waiting for transfers between devices, body(): lax.all_to_all(shaped_v, 'head', split_axis=2, concat_axis=0, tiled=True)  12.8 us
    all_to_all x1, waiting for transfers between devices, body(): lax.all_to_all(shaped_k, 'head', split_axis=2, concat_axis=0, tiled=True)  11.9 us
    all_to_all x1, starting transfers between devices, body(): lax.all_to_all(shaped_v, 'head', split_axis=2, concat_axis=0, tiled=True)  8.76 us
    gather x4, local copies, waits for them, and re-layouts, advance(): key_block = jnp.take(recv_k, block_items, axis=0)  8.65 us
    gather x4, local copies, waits for them, and re-layouts, advance(): value_block = jnp.take(recv_v, block_items, axis=0)  8.65 us
    all_to_all x1, starting transfers between devices, body(): lax.all_to_all(shaped_k, 'head', split_axis=2, concat_axis=0, tiled=True)  6.67 us
  transfers between devices with their start and end apart: 3, of which 3 were waited for; matrix products, arithmetic and copies ran while one was open for 2% of the time, Pallas kernels for 0%

commit v1 on v0

v1 whole, which is shorter than its diff:
```python
import functools
import math

import jax
import jax.numpy as jnp
from jax import lax
from jax.experimental import pallas as pl
from jax.experimental.pallas import tpu as pltpu
from jax.sharding import Mesh, PartitionSpec as P

Y_LO, X, Z = 2, 4, 8
Y_HI, CORE = 4, 2
COLUMNS = Y_LO * X
HEADS = Y_HI * CORE
HD = 128
PAGE = 128
MAXP = 16
PIECE = PAGE // COLUMNS
PLANE = ("y_lo", "x", "y_hi", "core")
COLUMN = ("y_lo", "x")
SMALL_CAP = 16
FULL_CAP = 64
HIDDEN = -1e30
EXP2_SCALE = math.log2(math.e) / math.sqrt(HD)
PARAMS = pltpu.CompilerParams(vmem_limit_bytes=40 * 2**20)
VMEM = pl.BlockSpec(memory_space=pltpu.VMEM)
SMEM = pl.BlockSpec(memory_space=pltpu.SMEM)


def split_kernel(key_ref, value_ref, out_ref):
    for page in range(out_ref.shape[1]):
        for kind, source in enumerate((key_ref, value_ref)):
            for column in range(COLUMNS):
                rows = pl.ds(column * PIECE, PIECE)
                for head in range(HEADS):
                    out_ref[column * HEADS + head, page, kind] = source[
                        page, rows, head * HD : (head + 1) * HD
                    ]


def split_pages(key_cache, value_cache):
    stored = key_cache.shape[0]
    return pl.pallas_call(
        split_kernel,
        out_shape=jax.ShapeDtypeStruct((COLUMNS * HEADS, stored, 2, PIECE, HD), jnp.bfloat16),
        in_specs=[VMEM, VMEM],
        out_specs=VMEM,
        compiler_params=PARAMS,
        name="split_pages",
    )(key_cache, value_cache)


def to_plane_kernel(table_ref, held_ref, out_ref):
    cap = out_ref.shape[1]
    for plane in range(Z):

        @pl.loop(0, cap, unroll=8)
        def _(place):
            out_ref[plane, place] = held_ref[table_ref[plane, place]]


def pick_for_planes(table, held):
    return pl.pallas_call(
        to_plane_kernel,
        out_shape=jax.ShapeDtypeStruct(table.shape + held.shape[1:], jnp.bfloat16),
        in_specs=[SMEM, VMEM],
        out_specs=VMEM,
        compiler_params=PARAMS,
        name="pick_for_planes",
    )(table, held)


def to_request_kernel(table_ref, held_ref, out_ref):
    for column in range(COLUMNS):

        @pl.loop(0, MAXP, unroll=8)
        def _(page):
            place = table_ref[column, page]
            out_ref[column, 0, page] = held_ref[place, 0]
            out_ref[column, 1, page] = held_ref[place, 1]


def pick_for_requests(table, held):
    return pl.pallas_call(
        to_request_kernel,
        out_shape=jax.ShapeDtypeStruct((COLUMNS, 2, MAXP, PIECE, HD), jnp.bfloat16),
        in_specs=[SMEM, VMEM],
        out_specs=VMEM,
        compiler_params=PARAMS,
        name="pick_for_requests",
    )(table, held)


HEADS_PER_STEP = 4


def contract_last(left, right):
    return lax.dot_general(
        left, right, (((1,), (1,)), ((), ())), preferred_element_type=jnp.float32
    )


def attend_kernel(length_ref, query_ref, key_ref, value_ref, held_ref, out_ref):
    tokens = query_ref.shape[0]
    group = query_ref.shape[1] // HD
    rows = HEADS_PER_STEP * tokens
    keys = MAXP * PIECE
    length = length_ref[0]
    at = lax.broadcasted_iota(jnp.int32, (1, keys), 1)
    position = (at // PIECE) * PAGE + at % PIECE
    biases = [
        jnp.where(position + column * PIECE < length, 0.0, HIDDEN) for column in range(COLUMNS)
    ]
    token = lax.broadcasted_iota(jnp.int32, (rows, tokens), 0) % tokens
    causal = lax.broadcasted_iota(jnp.int32, (rows, tokens), 1) <= token
    for step in range(group // HEADS_PER_STEP):
        first = step * HEADS_PER_STEP
        query = jnp.concatenate(
            [
                query_ref[:, (first + n) * HD : (first + n + 1) * HD]
                for n in range(HEADS_PER_STEP)
            ],
            axis=0,
        )
        fresh = jnp.where(causal, contract_last(query, key_ref[...]), HIDDEN)
        scores = [
            contract_last(query, held_ref[column, 0].reshape(keys, HD)) + biases[column]
            for column in range(COLUMNS)
        ]
        top = functools.reduce(jnp.maximum, scores)
        highest = jnp.maximum(
            jnp.max(top, axis=1, keepdims=True), jnp.max(fresh, axis=1, keepdims=True)
        )
        fresh = jnp.exp2((fresh - highest) * EXP2_SCALE)
        mixed = jnp.dot(
            fresh.astype(jnp.bfloat16), value_ref[...], preferred_element_type=jnp.float32
        )
        total = None
        for column in range(COLUMNS):
            weights = jnp.exp2((scores[column] - highest) * EXP2_SCALE)
            total = weights if total is None else total + weights
            mixed += jnp.dot(
                weights.astype(jnp.bfloat16),
                held_ref[column, 1].reshape(keys, HD),
                preferred_element_type=jnp.float32,
            )
        weight_sum = jnp.sum(total, axis=1, keepdims=True) + jnp.sum(
            fresh, axis=1, keepdims=True
        )
        mixed = (mixed / weight_sum).astype(jnp.bfloat16)
        for n in range(HEADS_PER_STEP):
            out_ref[:, (first + n) * HD : (first + n + 1) * HD] = mixed[
                n * tokens : (n + 1) * tokens
            ]


def attend(length, query, key_new, value_new, held):
    return pl.pallas_call(
        attend_kernel,
        out_shape=jax.ShapeDtypeStruct(query.shape, jnp.bfloat16),
        in_specs=[SMEM, VMEM, VMEM, VMEM, VMEM],
        out_specs=VMEM,
        compiler_params=PARAMS,
        name="attend",
    )(length, query, key_new, value_new, held)


def exchange(array, axes):
    return lax.all_to_all(array, axes, split_axis=0, concat_axis=0, tiled=True)


def by_plane(array):
    array = array.reshape(COLUMNS, Z, MAXP)
    return jnp.swapaxes(array, 0, 1).reshape(Z, COLUMNS * MAXP)


def routes(page_table, prefix_len):
    live = jnp.arange(MAXP, dtype=jnp.int32)[None, :] * PAGE < prefix_len[:, None]
    pages, live = by_plane(page_table), by_plane(live)
    from_plane = jnp.where(live, pages // MAXP % Z, -1)
    in_plane = pages // (MAXP * Z) * MAXP + pages % MAXP
    count = pages.shape[1]
    order = jnp.arange(count, dtype=jnp.int32)
    same = from_plane[:, :, None] == from_plane[:, None, :]
    earlier = order[None, :] < order[:, None]
    place = jnp.sum((same & earlier[None]).astype(jnp.int32), axis=2)
    place = jnp.where(live, place, -1)
    return from_plane, in_plane, place


def tail(cap, query, key_new, value_new, pieces, from_plane, in_plane, place, length):
    own_plane = lax.axis_index("z")
    wanted = jnp.arange(cap, dtype=jnp.int32)
    chosen = (from_plane == own_plane)[:, None, :] & (place[:, None, :] == wanted[None, :, None])
    plane_table = jnp.sum(jnp.where(chosen, in_plane[:, None, :], 0), axis=2)
    own_from = lax.dynamic_index_in_dim(from_plane, own_plane, 0, keepdims=False)
    own_place = lax.dynamic_index_in_dim(place, own_plane, 0, keepdims=False)
    slots = (own_from * cap + own_place).reshape(COLUMNS, MAXP)
    request_table = jnp.where(own_place.reshape(COLUMNS, MAXP) >= 0, slots, slots[:, :1])
    sent = pick_for_planes(plane_table, pieces)
    gathered = exchange(sent, "z").reshape((Z * cap,) + pieces.shape[1:])
    ready = pick_for_requests(request_table, gathered)
    held = exchange(ready, COLUMN)
    return attend(length, query, key_new, value_new, held)


def body(query, key_new, value_new, key_cache, value_cache, page_table, prefix_len):
    own_request = lax.axis_index(("y_lo", "x", "z"))
    pieces = exchange(split_pages(key_cache, value_cache), PLANE)
    pieces = pieces.reshape((COLUMNS * MAXP,) + pieces.shape[2:])
    from_plane, in_plane, place = routes(page_table, prefix_len)
    length = lax.dynamic_slice_in_dim(prefix_len, own_request, 1)
    operands = (query, key_new, value_new, pieces, from_plane, in_plane, place, length)
    return lax.cond(
        jnp.max(place) < SMALL_CAP,
        functools.partial(tail, SMALL_CAP),
        functools.partial(tail, FULL_CAP),
        *operands,
    )


def solution(mesh):
    fine = Mesh(
        mesh.devices.reshape(Y_LO, X, Z, Y_HI, CORE), ("y_lo", "x", "z", "y_hi", "core")
    )
    wide, head = ("y_lo", "x", "z"), ("y_hi", "core")
    in_specs = (
        P(wide, head),
        P(wide, head),
        P(wide, head),
        P(wide + head, None, None),
        P(wide + head, None, None),
        P(),
        P(),
    )
    return jax.shard_map(
        body, mesh=fine, in_specs=in_specs, out_specs=P(wide, head), check_vma=False
    )
```

time: 204 us -> 111 us (0.54)
  the two profiles are of different devices: /device:TPU:24 before, /device:TPU:1 now
where the time goes in v1:
time: 111 us
  waiting for transfers between devices  69.7 us (63%)
  starting transfers between devices  25.2 us (23%)
  Pallas kernels  9.64 us (9%)
  local copies, waits for them, and re-layouts  4.31 us (4%)
  other arithmetic  1.4 us (1%)
    all_to_all x3, waiting for transfers between devices, exchange(): return lax.all_to_all(array, axes, split_axis=0, concat_axis=0, tiled=True)  69.7 us
    all_to_all x3, starting transfers between devices, exchange(): return lax.all_to_all(array, axes, split_axis=0, concat_axis=0, tiled=True)  25.2 us
    pallas_call x1, Pallas kernels, attend(): pl.pallas_call(attend_kernel, out_shape=jax.ShapeDtypeStruct(query.shape,...  4.55 us
    unnamed x17, local copies, waits for them, and re-layouts  2.88 us
  transfers between devices with their start and end apart: 3, of which 3 were waited for; matrix products, arithmetic and copies ran while one was open for 2% of the time, Pallas kernels for 0%

profile of v1, /device:TPU:1, one launch (start us, length us, event | category | flops | bytes accessed | tf_op | source)
XLA Modules:
  0.0 111.0 jit_solution(1476309990412620523)
XLA Ops:
  0.0 0.0 copy-start.1
  0.0 1.0 copy-done.1
  1.0 0.0 copy-start.2
  1.0 1.0 copy-done.2
  2.1 0.0 copy-start.7
  2.1 0.0 copy-start.8
  2.1 0.0 copy-start.3
  2.1 0.0 copy-start.5
  2.1 0.0 copy-start.6
  2.1 1.2 %split_pages.1 = bf16[64,2,2,16,128]{4,3,2,1,0:T(8,128)(2,1)} custom-call(bf16[2,128,1024]{2,1,0:T(8,128)(2,1)S(1)} %copy-done.1, bf16[2,128,1024]{2,1,0:T(8,128)(2,1)S(1)} %copy-done.2), custom_call_target="tpu_custom_call" | custom-call | tf_op jit(solution)/shard_map/split_pages/pallas_call | solution.py:43
  3.3 11.6 %all-to-all-start.4 = ((bf16[64,2,2,16,128]{4,3,2,1,0:T(8,128)(2,1)}), bf16[64,2,2,16,128]{4,3,2,1,0:T(8,128)(2,1)S(1)}, u32[]{:S(2)}, u32[]{:S(2)}) async-start(bf16[64,2,2,16,128]{4,3,2,1,0:T(8,128)(2,1)} %split_pages.1), calls=%async_computation.4 | async-start | bytes 2097152 | tf_op jit(solution)/shard_map/all_to_all | solution.py:169
  14.9 0.0 copy-done.7
  14.9 0.1 copy.18
  15.0 0.1 reshape.193
  15.1 0.0 copy-done.8
  15.1 0.1 lt.86
  15.2 0.1 copy.17
  15.2 0.1 lt.88
  15.3 0.1 lt.89
  15.4 0.1 lt.84
  15.6 0.4 convert_reduce_fusion
  15.9 0.6 select_reduce_fusion.2
  17.2 26.7 %all-to-all-done.4 = bf16[64,2,2,16,128]{4,3,2,1,0:T(8,128)(2,1)S(1)} async-done(((bf16[64,2,2,16,128]{4,3,2,1,0:T(8,128)(2,1)}), bf16[64,2,2,16,128]{4,3,2,1,0:T(8,128)(2,1)S(1)}, u32[]{:S(2)}, u32[]{:S(2)}) %all-to-all-start.4) | async-done | bytes 1048608 | tf_op jit(solution)/shard_map/all_to_all | solution.py:169
  43.9 0.0 copy-done.3
  43.9 0.0 copy-done.5
  43.9 0.0 copy-done.6
  43.9 66.4 %conditional.1 = (bf16[64,2048]{1,0:T(8,128)(2,1)S(1)}) conditional(s32[]{:T(128)} %convert_element_type.7, (s32[]{:T(128)}, s32[]{:T(128)}, s32[]{:T(128)}, s32[64]{0:T(128)S(1)}, pred[8,128]{1,0:T(8,128)(4,1)S(1)}, /*index=5*/s32[8,128]{1,0:T(8,128)S(1)}, s32[8,128]{1,0:T(8,128)S(1)}, s32[8,128]{1,0:T(8,128)S(1)}, s32[8,128]{1,0:T(8,128)S(1)}, ...), branch_computations={%region_2.4_spmd, %region_4.6_spmd} | conditional | flops 280589 | bytes 32559984 | solution.py:214
  44.0 0.2 select_reduce_fusion.1.table_ref
  44.2 2.0 %pick_for_planes.3 = bf16[8,16,2,16,128]{4,3,2,1,0:T(8,128)(2,1)} custom-call(s32[8,16]{1,0:T(8,128)S(1)} %select_reduce_fusion.1.table_ref, bf16[128,2,16,128]{3,2,1,0:T(8,128)(2,1)S(1)} %bitcast.10), custom_call_target="tpu_custom_call" | custom-call | tf_op jit(solution)/shard_map/cond/branch_1_fun/pick_for_planes/pallas_call | solution.py:63
  46.1 10.0 %all-to-all-start.2 = ((bf16[8,16,2,16,128]{4,3,2,1,0:T(8,128)(2,1)}), bf16[8,16,2,16,128]{4,3,2,1,0:T(8,128)(2,1)S(1)}, u32[]{:S(2)}, u32[]{:S(2)}) async-start(bf16[8,16,2,16,128]{4,3,2,1,0:T(8,128)(2,1)} %pick_for_planes.3), calls=%async_computation.2 | async-start | bytes 2097152 | tf_op jit(solution)/shard_map/cond/branch_1_fun/all_to_all | solution.py:169
  56.2 0.1 add.81
  56.3 0.1 ge.11
  56.4 0.1 slice_reduce_fusion.1
  56.5 0.1 broadcast_select_fusion.1.table_ref
  56.6 28.8 %all-to-all-done.2 = bf16[8,16,2,16,128]{4,3,2,1,0:T(8,128)(2,1)S(1)} async-done(((bf16[8,16,2,16,128]{4,3,2,1,0:T(8,128)(2,1)}), bf16[8,16,2,16,128]{4,3,2,1,0:T(8,128)(2,1)S(1)}, u32[]{:S(2)}, u32[]{:S(2)}) %all-to-all-start.2) | async-done | bytes 1048608 | tf_op jit(solution)/shard_map/cond/branch_1_fun/all_to_all | solution.py:169
  85.4 2.0 %pick_for_requests.3 = bf16[8,2,16,16,128]{4,3,2,1,0:T(8,128)(2,1)} custom-call(s32[8,16]{1,0:T(8,128)S(1)} %broadcast_select_fusion.1.table_ref, bf16[128,2,16,128]{3,2,1,0:T(8,128)(2,1)S(1)} %bitcast.8), custom_call_target="tpu_custom_call" | custom-call | tf_op jit(solution)/shard_map/cond/branch_1_fun/pick_for_requests/pallas_call | solution.py:84
  87.3 3.6 %all-to-all-start.3 = ((bf16[8,2,16,16,128]{4,3,2,1,0:T(8,128)(2,1)}), bf16[8,2,16,16,128]{4,3,2,1,0:T(8,128)(2,1)S(1)}, u32[]{:S(2)}, u32[]{:S(2)}) async-start(bf16[8,2,16,16,128]{4,3,2,1,0:T(8,128)(2,1)} %pick_for_requests.3), calls=%async_computation.3 | async-start | bytes 2097152 | tf_op jit(solution)/shard_map/cond/branch_1_fun/all_to_all | solution.py:169
  90.9 0.7 dynamic_slice.17.length_ref
  91.6 14.2 %all-to-all-done.3.held_ref = bf16[8,2,16,16,128]{4,3,2,1,0:T(8,128)(2,1)S(1)} async-done(((bf16[8,2,16,16,128]{4,3,2,1,0:T(8,128)(2,1)}), bf16[8,2,16,16,128]{4,3,2,1,0:T(8,128)(2,1)S(1)}, u32[]{:S(2)}, u32[]{:S(2)}) %all-to-all-start.3) | async-done | bytes 1048608 | tf_op jit(solution)/shard_map/cond/branch_1_fun/all_to_all | solution.py:169
  105.8 4.6 %attend.3 = bf16[64,2048]{1,0:T(8,128)(2,1)S(1)} custom-call(s32[1]{0:T(128)} %dynamic_slice.17.length_ref, bf16[64,2048]{1,0:T(8,128)(2,1)S(1)} %get-tuple-element.198.query_ref, bf16[64,128]{1,0:T(8,128)(2,1)S(1)} %get-tuple-element.199.key_ref, bf16[64,128]{1,0:T(8,128)(2,1)S(1)} %get-tuple-element.200.value_ref, ...), custom_call_target="tpu_custom_call" | custom-call | tf_op jit(solution)/shard_map/cond/branch_1_fun/attend/pallas_call | solution.py:158
  110.3 0.0 copy-start.4
  110.3 0.7 copy-done.4
  (11 shorter events, 0.1 us)
Async XLA Ops:
  0.0 1.0 copy-start.1
  1.0 1.0 copy-start.2
  2.1 12.8 %copy-start.7 = (s32[64,16]{0,1:T(8,128)S(1)}, s32[64,16]{0,1:T(8,128)}, u32[]{:S(2)}) copy-start(s32[64,16]{0,1:T(8,128)} %param.14) | copy-start | bytes 12292
  2.1 13.0 %copy-start.8 = (s32[64]{0:T(128)S(1)}, s32[64]{0:T(128)}, u32[]{:S(2)}) copy-start(s32[64]{0:T(128)} %param.15) | copy-start | bytes 772
  2.1 41.8 %copy-start.3 = (bf16[64,2048]{1,0:T(8,128)(2,1)S(1)}, bf16[64,2048]{1,0:T(8,128)(2,1)}, u32[]{:S(2)}) copy-start(bf16[64,2048]{1,0:T(8,128)(2,1)} %param.9) | copy-start | bytes 786436
  2.1 41.8 %copy-start.5 = (bf16[64,128]{1,0:T(8,128)(2,1)S(1)}, bf16[64,128]{1,0:T(8,128)(2,1)}, u32[]{:S(2)}) copy-start(bf16[64,128]{1,0:T(8,128)(2,1)} %param.10) | copy-start | bytes 49156
  2.1 41.8 %copy-start.6 = (bf16[64,128]{1,0:T(8,128)(2,1)S(1)}, bf16[64,128]{1,0:T(8,128)(2,1)}, u32[]{:S(2)}) copy-start(bf16[64,128]{1,0:T(8,128)(2,1)} %param.11) | copy-start | bytes 49156
  3.3 40.6 %all-to-all-start.4 = ((bf16[64,2,2,16,128]{4,3,2,1,0:T(8,128)(2,1)}), bf16[64,2,2,16,128]{4,3,2,1,0:T(8,128)(2,1)S(1)}, u32[]{:S(2)}, u32[]{:S(2)}) async-start(bf16[64,2,2,16,128]{4,3,2,1,0:T(8,128)(2,1)} %split_pages.1), calls=%async_computation.4 | async-start | bytes 2097152 | tf_op jit(solution)/shard_map/all_to_all | solution.py:169
  46.1 39.2 %all-to-all-start.2 = ((bf16[8,16,2,16,128]{4,3,2,1,0:T(8,128)(2,1)}), bf16[8,16,2,16,128]{4,3,2,1,0:T(8,128)(2,1)S(1)}, u32[]{:S(2)}, u32[]{:S(2)}) async-start(bf16[8,16,2,16,128]{4,3,2,1,0:T(8,128)(2,1)} %pick_for_planes.3), calls=%async_computation.2 | async-start | bytes 2097152 | tf_op jit(solution)/shard_map/cond/branch_1_fun/all_to_all | solution.py:169
  87.3 18.5 %all-to-all-start.3 = ((bf16[8,2,16,16,128]{4,3,2,1,0:T(8,128)(2,1)}), bf16[8,2,16,16,128]{4,3,2,1,0:T(8,128)(2,1)S(1)}, u32[]{:S(2)}, u32[]{:S(2)}) async-start(bf16[8,2,16,16,128]{4,3,2,1,0:T(8,128)(2,1)} %pick_for_requests.3), calls=%async_computation.3 | async-start | bytes 2097152 | tf_op jit(solution)/shard_map/cond/branch_1_fun/all_to_all | solution.py:169
  110.3 0.7 copy-start.4

commit v2 on v1

v2 whole, which is shorter than its diff:
```python
import functools
import math

import jax
import jax.numpy as jnp
from jax import lax
from jax.experimental import pallas as pl
from jax.experimental.pallas import tpu as pltpu
from jax.sharding import Mesh, PartitionSpec as P

Y_LO, X, Z = 2, 4, 8
Y_HI, CORE = 4, 2
WIDE_AXES, HEAD_AXES = ("y_lo", "x", "z"), ("y_hi", "core")
WIDE = Y_LO * X * Z
HEADS = Y_HI * CORE
HD = 128
PAGE = 128
MAXP = 16
STORED = 2
PIECE = PAGE // WIDE
ROWS = STORED * 2 * PIECE
HIDDEN = -1e30
EXP2_SCALE = math.log2(math.e) / math.sqrt(HD)
PARAMS = pltpu.CompilerParams(vmem_limit_bytes=40 * 2**20)
VMEM = pl.BlockSpec(memory_space=pltpu.VMEM)
SMEM = pl.BlockSpec(memory_space=pltpu.SMEM)
HBM = pl.BlockSpec(memory_space=pltpu.HBM)

PARTS = 4
PART_TOKENS = PAGE // PARTS
PART_WIDE = WIDE // PARTS


def split_kernel(key_hbm, value_hbm, out_hbm, cache, ready, in_sems, out_sems):
    def fetch(part, kind):
        tokens = pl.ds(part * PART_TOKENS, PART_TOKENS)
        source = (key_hbm, value_hbm)[kind]
        return pltpu.make_async_copy(
            source.at[:, tokens], cache.at[kind, :, tokens], in_sems.at[part, kind]
        )

    def leave(part):
        rows = pl.ds(part * PART_WIDE, PART_WIDE)
        return pltpu.make_async_copy(ready.at[rows], out_hbm.at[rows], out_sems.at[part])

    for part in range(PARTS):
        for kind in range(2):
            fetch(part, kind).start()
    count = PART_WIDE * ROWS
    at = lax.broadcasted_iota(jnp.int32, (count, count), 0)
    source_row = (at % ROWS // PIECE) * PART_TOKENS + at // ROWS * PIECE + at % PIECE
    moved = source_row == lax.broadcasted_iota(jnp.int32, (count, count), 1)
    moved = jnp.where(moved, 1.0, 0.0).astype(jnp.bfloat16)
    for part in range(PARTS):
        for kind in range(2):
            fetch(part, kind).wait()
        tokens = slice(part * PART_TOKENS, (part + 1) * PART_TOKENS)
        rows = jnp.concatenate(
            [cache[kind, page, tokens] for page in range(STORED) for kind in range(2)], axis=0
        )
        rows = jnp.dot(moved, rows, preferred_element_type=jnp.float32)
        for pair in range(HEADS // 2):
            both = [
                rows[:, head * HD : (head + 1) * HD].reshape(PART_WIDE, ROWS, HD)
                for head in (2 * pair, 2 * pair + 1)
            ]
            ready[part * PART_WIDE : (part + 1) * PART_WIDE, pair] = jnp.concatenate(
                both, axis=1
            ).astype(jnp.bfloat16)
        leave(part).start()
    for part in range(PARTS):
        leave(part).wait()


def split_pages(key_cache, value_cache):
    shape = (WIDE, HEADS // 2, 2 * ROWS, HD)
    return pl.pallas_call(
        split_kernel,
        out_shape=jax.ShapeDtypeStruct(shape, jnp.bfloat16),
        in_specs=[HBM, HBM],
        out_specs=HBM,
        scratch_shapes=[
            pltpu.VMEM((2,) + key_cache.shape, jnp.bfloat16),
            pltpu.VMEM(shape, jnp.bfloat16),
            pltpu.SemaphoreType.DMA((PARTS, 2)),
            pltpu.SemaphoreType.DMA((PARTS,)),
        ],
        compiler_params=PARAMS,
        name="split_pages",
    )(key_cache, value_cache)


PICK_REQUESTS = 16


def pick_kernel(chosen_ref, held_ref, out_ref, spread):
    sources = held_ref.shape[0] * 2
    spread[...] = held_ref[...].reshape(sources * ROWS, HD).astype(jnp.float32)
    columns = []
    for quarter in range(2 * PIECE):
        column = [
            spread[pl.ds(page * 2 * PIECE + quarter, sources, stride=ROWS), :]
            for page in range(STORED)
        ]
        columns.append(jnp.concatenate(column, axis=0).astype(jnp.bfloat16))
    columns = jnp.concatenate(columns, axis=1)
    for step in range(WIDE // PICK_REQUESTS):
        first = step * PICK_REQUESTS
        picked = jnp.dot(
            chosen_ref[first * MAXP : (first + PICK_REQUESTS) * MAXP],
            columns,
            preferred_element_type=jnp.float32,
        ).astype(jnp.bfloat16)
        for request in range(PICK_REQUESTS):
            for quarter in range(2 * PIECE):
                out_ref[first + request, quarter * MAXP : (quarter + 1) * MAXP] = picked[
                    request * MAXP : (request + 1) * MAXP, quarter * HD : (quarter + 1) * HD
                ]


def pick_pages(chosen, held):
    shape = (WIDE, 2 * PIECE * MAXP, HD)
    return pl.pallas_call(
        pick_kernel,
        out_shape=jax.ShapeDtypeStruct(shape, jnp.bfloat16),
        in_specs=[VMEM, VMEM],
        out_specs=VMEM,
        scratch_shapes=[pltpu.VMEM((held.shape[0] * 2 * ROWS, HD), jnp.float32)],
        compiler_params=PARAMS,
        name="pick_pages",
    )(chosen, held)


HEADS_PER_STEP = 4
CHUNK_WIDE = 8


def contract_last(left, right):
    return lax.dot_general(
        left, right, (((1,), (1,)), ((), ())), preferred_element_type=jnp.float32
    )


def attend_kernel(length_ref, query_ref, key_ref, value_ref, held_ref, out_ref):
    tokens = query_ref.shape[0]
    group = query_ref.shape[1] // HD
    rows = HEADS_PER_STEP * tokens
    half = PIECE * MAXP
    keys = CHUNK_WIDE * half
    chunks = WIDE // CHUNK_WIDE
    length = length_ref[0]
    at = lax.broadcasted_iota(jnp.int32, (1, keys), 1)
    position = at % MAXP * PAGE + at // MAXP
    biases = [
        jnp.where(position + chunk * CHUNK_WIDE * PIECE < length, 0.0, HIDDEN)
        for chunk in range(chunks)
    ]
    token = lax.broadcasted_iota(jnp.int32, (rows, tokens), 0) % tokens
    causal = lax.broadcasted_iota(jnp.int32, (rows, tokens), 1) <= token

    def held(chunk, kind):
        block = held_ref[
            chunk * CHUNK_WIDE : (chunk + 1) * CHUNK_WIDE, kind * half : (kind + 1) * half
        ]
        return block.reshape(keys, HD)

    for step in range(group // HEADS_PER_STEP):
        first = step * HEADS_PER_STEP
        query = jnp.concatenate(
            [
                query_ref[:, (first + n) * HD : (first + n + 1) * HD]
                for n in range(HEADS_PER_STEP)
            ],
            axis=0,
        )
        fresh = jnp.where(causal, contract_last(query, key_ref[...]), HIDDEN)
        scores = [
            contract_last(query, held(chunk, 0)) + biases[chunk] for chunk in range(chunks)
        ]
        top = functools.reduce(jnp.maximum, scores)
        highest = jnp.maximum(
            jnp.max(top, axis=1, keepdims=True), jnp.max(fresh, axis=1, keepdims=True)
        )
        fresh = jnp.exp2((fresh - highest) * EXP2_SCALE)
        mixed = jnp.dot(
            fresh.astype(jnp.bfloat16), value_ref[...], preferred_element_type=jnp.float32
        )
        total = None
        for chunk in range(chunks):
            weights = jnp.exp2((scores[chunk] - highest) * EXP2_SCALE)
            total = weights if total is None else total + weights
            mixed += jnp.dot(
                weights.astype(jnp.bfloat16), held(chunk, 1), preferred_element_type=jnp.float32
            )
        weight_sum = jnp.sum(total, axis=1, keepdims=True) + jnp.sum(
            fresh, axis=1, keepdims=True
        )
        mixed = (mixed / weight_sum).astype(jnp.bfloat16)
        for n in range(HEADS_PER_STEP):
            out_ref[:, (first + n) * HD : (first + n + 1) * HD] = mixed[
                n * tokens : (n + 1) * tokens
            ]


def attend(length, query, key_new, value_new, held):
    return pl.pallas_call(
        attend_kernel,
        out_shape=jax.ShapeDtypeStruct(query.shape, jnp.bfloat16),
        in_specs=[SMEM, VMEM, VMEM, VMEM, VMEM],
        out_specs=VMEM,
        compiler_params=PARAMS,
        name="attend",
    )(length, query, key_new, value_new, held)


def exchange(array, axes):
    return lax.all_to_all(array, axes, split_axis=0, concat_axis=0, tiled=True)


def body(query, key_new, value_new, key_cache, value_cache, page_table, prefix_len):
    own_request = lax.axis_index(WIDE_AXES)
    length = lax.dynamic_slice_in_dim(prefix_len, own_request, 1)
    sources = WIDE * HEADS
    pages = page_table.reshape(-1)
    column = pages % STORED * sources + pages // STORED
    every = jnp.arange(STORED * sources, dtype=jnp.int32)
    chosen = (column[:, None] == every[None, :]).astype(jnp.bfloat16)
    pieces = split_pages(key_cache, value_cache).reshape(sources, ROWS, HD)
    pieces = exchange(pieces, WIDE_AXES + HEAD_AXES)
    picked = pick_pages(chosen, pieces.reshape(sources // 2, 2 * ROWS, HD))
    held = exchange(picked, WIDE_AXES)
    return attend(length, query, key_new, value_new, held)


def solution(mesh):
    fine = Mesh(mesh.devices.reshape(Y_LO, X, Z, Y_HI, CORE), WIDE_AXES + HEAD_AXES)
    in_specs = (
        P(WIDE_AXES, HEAD_AXES),
        P(WIDE_AXES, HEAD_AXES),
        P(WIDE_AXES, HEAD_AXES),
        P(WIDE_AXES + HEAD_AXES, None, None),
        P(WIDE_AXES + HEAD_AXES, None, None),
        P(),
        P(),
    )
    return jax.shard_map(
        body,
        mesh=fine,
        in_specs=in_specs,
        out_specs=P(WIDE_AXES, HEAD_AXES),
        check_vma=False,
    )
```

time: 111 us -> 102 us (0.919); the launches traced: 111 us -> 101 us
  waiting for transfers between devices: 69.7 us -> 59.4 us
  starting transfers between devices: 25.2 us -> 27.8 us
  local copies, waits for them, and re-layouts: 4.31 us -> 2.87 us
    all_to_all x3 -> x2, waiting for transfers between devices: 69.7 us -> 59.4 us  [exchange(): return lax.all_to_all(array, axes, split_axis=0, concat_axis=0, tiled=True)]
    all_to_all x3 -> x2, starting transfers between devices: 25.2 us -> 27.8 us  [exchange(): return lax.all_to_all(array, axes, split_axis=0, concat_axis=0, tiled=True)]
    unnamed x17 -> x15, local copies, waits for them, and re-layouts: 2.88 us -> 2.18 us
    pallas_call x3 -> x2, Pallas kernels: 5.09 us -> 4.9 us  [the longest x1 2.53 us: pick_pages(): pl.pallas_call(pick_kernel, out_shape=jax.ShapeDtypeStruct(shape, jnp.bfl...]
  transfers between devices with their start and end apart: 3 -> 2, of which waited for: 3 -> 2; matrix products, arithmetic and copies ran while one was open for 2% -> 1% of each run, Pallas kernels for 0% -> 0%
where the time goes in v2:
time: 102 us; the launch traced here: 101 us
  waiting for transfers between devices  59.4 us (58%)
  starting transfers between devices  27.8 us (27%)
  Pallas kernels  10.1 us (10%)
  local copies, waits for them, and re-layouts  2.87 us (3%)
    all_to_all x2, waiting for transfers between devices, exchange(): return lax.all_to_all(array, axes, split_axis=0, concat_axis=0, tiled=True)  59.4 us
    all_to_all x2, starting transfers between devices, exchange(): return lax.all_to_all(array, axes, split_axis=0, concat_axis=0, tiled=True)  27.8 us
    pallas_call x1, Pallas kernels, attend(): pl.pallas_call(attend_kernel, out_shape=jax.ShapeDtypeStruct(query.shape,...  5.18 us
    pallas_call x1, Pallas kernels, pick_pages(): pl.pallas_call(pick_kernel, out_shape=jax.ShapeDtypeStruct(shape, jnp.bfl...  2.53 us
    pallas_call x1, Pallas kernels, split_pages(): pl.pallas_call(split_kernel, out_shape=jax.ShapeDtypeStruct(shape, jnp.bf...  2.38 us
    unnamed x15, local copies, waits for them, and re-layouts  2.18 us
  transfers between devices with their start and end apart: 2, of which 2 were waited for; matrix products, arithmetic and copies ran while one was open for 1% of the time, Pallas kernels for 0%

profile of v2, /device:TPU:1, one launch (start us, length us, event | category | flops | bytes accessed | tf_op | source)
XLA Modules:
  0.0 100.7 jit_solution(18136800613711740450)
XLA Ops:
  0.0 0.0 copy-start
  0.0 1.0 %copy-done = bf16[2,128,1024]{2,1,0:T(8,128)(2,1)S(1)} copy-done((bf16[2,128,1024]{2,1,0:T(8,128)(2,1)S(1)}, bf16[2,128,1024]{2,1,0:T(8,128)(2,1)}, u32[]{:S(2)}) %copy-start) | copy-done | bytes 524312
  1.0 0.0 copy-start.1
  1.0 1.0 %copy-done.1 = bf16[2,128,1024]{2,1,0:T(8,128)(2,1)S(1)} copy-done((bf16[2,128,1024]{2,1,0:T(8,128)(2,1)S(1)}, bf16[2,128,1024]{2,1,0:T(8,128)(2,1)}, u32[]{:S(2)}) %copy-start.1) | copy-done | bytes 524312
  2.1 0.0 copy-start.5
  2.1 2.4 %split_pages.1 = bf16[64,4,16,128]{3,2,1,0:T(8,128)(2,1)} custom-call(bf16[2,128,1024]{2,1,0:T(8,128)(2,1)S(1)} %copy-done, bf16[2,128,1024]{2,1,0:T(8,128)(2,1)S(1)} %copy-done.1), custom_call_target="tpu_custom_call" | custom-call | tf_op jit(solution)/shard_map/split_pages/pallas_call | solution.py:77
  4.5 22.2 %all-to-all-start = ((bf16[512,8,128]{2,1,0:T(8,128)(2,1)}), bf16[512,8,128]{2,1,0:T(8,128)(2,1)S(1)}, u32[]{:S(2)}, u32[]{:S(2)}) async-start(bf16[512,8,128]{2,1,0:T(8,128)(2,1)} %bitcast), calls=%async_computation | async-start | bytes 2097152 | tf_op jit(solution)/shard_map/all_to_all | solution.py:217
  26.6 0.0 copy-done.5
  26.7 0.1 copy.8
  26.7 0.1 reshape.59
  26.8 0.4 fusion.chosen_ref
  27.3 31.8 %all-to-all-done = bf16[512,8,128]{2,1,0:T(8,128)(2,1)S(1)} async-done(((bf16[512,8,128]{2,1,0:T(8,128)(2,1)}), bf16[512,8,128]{2,1,0:T(8,128)(2,1)S(1)}, u32[]{:S(2)}, u32[]{:S(2)}) %all-to-all-start) | async-done | bytes 1048608 | tf_op jit(solution)/shard_map/all_to_all | solution.py:217
  59.1 2.5 %pick_pages.1 = bf16[64,64,128]{2,1,0:T(8,128)(2,1)} custom-call(bf16[1024,1024]{1,0:T(8,128)(2,1)S(1)} %fusion.chosen_ref, bf16[256,16,128]{2,1,0:T(8,128)(2,1)S(1)} %bitcast.2), custom_call_target="tpu_custom_call" | custom-call | tf_op jit(solution)/shard_map/pick_pages/pallas_call | solution.py:123
  61.6 0.0 copy-start.6
  61.6 0.0 copy-start.2
  61.6 0.0 copy-start.3
  61.6 0.0 copy-start.4
  61.6 5.7 %all-to-all-start.1 = ((bf16[64,64,128]{2,1,0:T(8,128)(2,1)}), bf16[64,64,128]{2,1,0:T(8,128)(2,1)S(1)}, u32[]{:S(2)}, u32[]{:S(2)}) async-start(bf16[64,64,128]{2,1,0:T(8,128)(2,1)} %pick_pages.1), calls=%async_computation.1 | async-start | bytes 2097152 | tf_op jit(solution)/shard_map/all_to_all | solution.py:217
  67.3 0.0 copy-done.6
  67.3 0.6 dynamic_slice.3.length_ref
  67.9 27.6 %all-to-all-done.1.held_ref = bf16[64,64,128]{2,1,0:T(8,128)(2,1)S(1)} async-done(((bf16[64,64,128]{2,1,0:T(8,128)(2,1)}), bf16[64,64,128]{2,1,0:T(8,128)(2,1)S(1)}, u32[]{:S(2)}, u32[]{:S(2)}) %all-to-all-start.1) | async-done | bytes 1048608 | tf_op jit(solution)/shard_map/all_to_all | solution.py:217
  95.5 0.0 copy-done.2
  95.5 0.0 copy-done.3
  95.5 0.0 copy-done.4
  95.5 5.2 %attend.1 = bf16[64,2048]{1,0:T(8,128)(2,1)} custom-call(s32[1]{0:T(128)} %dynamic_slice.3.length_ref, bf16[64,2048]{1,0:T(8,128)(2,1)S(1)} %copy-done.2, bf16[64,128]{1,0:T(8,128)(2,1)S(1)} %copy-done.3, bf16[64,128]{1,0:T(8,128)(2,1)S(1)} %copy-done.4, bf16[64,64,128]{2,1,0:T(8,128)(2,1)S(1)} %all-to-all-done.1.held_ref), custom_call_target="tpu_custom_call" | custom-call | tf_op jit(solution)/shard_map/attend/pallas_call | solution.py:206
  (1 shorter events, 0.0 us)
Async XLA Ops:
  0.0 1.0 %copy-start = (bf16[2,128,1024]{2,1,0:T(8,128)(2,1)S(1)}, bf16[2,128,1024]{2,1,0:T(8,128)(2,1)}, u32[]{:S(2)}) copy-start(bf16[2,128,1024]{2,1,0:T(8,128)(2,1)} %key_hbm.1) | copy-start | bytes 1572868
  1.0 1.0 %copy-start.1 = (bf16[2,128,1024]{2,1,0:T(8,128)(2,1)S(1)}, bf16[2,128,1024]{2,1,0:T(8,128)(2,1)}, u32[]{:S(2)}) copy-start(bf16[2,128,1024]{2,1,0:T(8,128)(2,1)} %value_hbm.1) | copy-start | bytes 1572868
  2.1 24.6 %copy-start.5 = (s32[64,16]{0,1:T(8,128)S(1)}, s32[64,16]{0,1:T(8,128)}, u32[]{:S(2)}) copy-start(s32[64,16]{0,1:T(8,128)} %param.12) | copy-start | bytes 12292
  4.5 54.6 %all-to-all-start = ((bf16[512,8,128]{2,1,0:T(8,128)(2,1)}), bf16[512,8,128]{2,1,0:T(8,128)(2,1)S(1)}, u32[]{:S(2)}, u32[]{:S(2)}) async-start(bf16[512,8,128]{2,1,0:T(8,128)(2,1)} %bitcast), calls=%async_computation | async-start | bytes 2097152 | tf_op jit(solution)/shard_map/all_to_all | solution.py:217
  61.6 5.7 %copy-start.6 = (s32[64]{0:T(128)S(1)}, s32[64]{0:T(128)}, u32[]{:S(2)}) copy-start(s32[64]{0:T(128)} %param.13) | copy-start | bytes 772
  61.6 33.9 %copy-start.2 = (bf16[64,2048]{1,0:T(8,128)(2,1)S(1)}, bf16[64,2048]{1,0:T(8,128)(2,1)}, u32[]{:S(2)}) copy-start(bf16[64,2048]{1,0:T(8,128)(2,1)} %query_ref.1) | copy-start | bytes 786436
  61.6 33.9 %copy-start.3 = (bf16[64,128]{1,0:T(8,128)(2,1)S(1)}, bf16[64,128]{1,0:T(8,128)(2,1)}, u32[]{:S(2)}) copy-start(bf16[64,128]{1,0:T(8,128)(2,1)} %key_ref.1) | copy-start | bytes 49156
  61.6 33.9 %copy-start.4 = (bf16[64,128]{1,0:T(8,128)(2,1)S(1)}, bf16[64,128]{1,0:T(8,128)(2,1)}, u32[]{:S(2)}) copy-start(bf16[64,128]{1,0:T(8,128)(2,1)} %value_ref.1) | copy-start | bytes 49156
  61.6 33.9 %all-to-all-start.1 = ((bf16[64,64,128]{2,1,0:T(8,128)(2,1)}), bf16[64,64,128]{2,1,0:T(8,128)(2,1)S(1)}, u32[]{:S(2)}, u32[]{:S(2)}) async-start(bf16[64,64,128]{2,1,0:T(8,128)(2,1)} %pick_pages.1), calls=%async_computation.1 | async-start | bytes 2097152 | tf_op jit(solution)/shard_map/all_to_all | solution.py:217

commit v3 on v2

--- a/solution.py
+++ b/solution.py
@@ -22,11 +22,11 @@
 HIDDEN = -1e30
 EXP2_SCALE = math.log2(math.e) / math.sqrt(HD)
 PARAMS = pltpu.CompilerParams(vmem_limit_bytes=40 * 2**20)
+ALL_PARAMS = pltpu.CompilerParams(vmem_limit_bytes=63 * 2**20)
 VMEM = pl.BlockSpec(memory_space=pltpu.VMEM)
-SMEM = pl.BlockSpec(memory_space=pltpu.SMEM)
 HBM = pl.BlockSpec(memory_space=pltpu.HBM)
 
-PARTS = 4
+PARTS = 2
 PART_TOKENS = PAGE // PARTS
 PART_WIDE = WIDE // PARTS
 
@@ -85,16 +85,22 @@
             pltpu.SemaphoreType.DMA((PARTS, 2)),
             pltpu.SemaphoreType.DMA((PARTS,)),
         ],
-        compiler_params=PARAMS,
+        compiler_params=ALL_PARAMS,
         name="split_pages",
     )(key_cache, value_cache)
 
 
-PICK_REQUESTS = 16
-
-
-def pick_kernel(chosen_ref, held_ref, out_ref, spread):
+PICK_REQUESTS = 32
+PICK_STEPS = WIDE // PICK_REQUESTS
+
+
+def pick_kernel(chosen_ref, held_ref, out_hbm, spread, ready, sems):
     sources = held_ref.shape[0] * 2
+
+    def leave(step):
+        requests = pl.ds(step * PICK_REQUESTS, PICK_REQUESTS)
+        return pltpu.make_async_copy(ready.at[requests], out_hbm.at[requests], sems.at[step])
+
     spread[...] = held_ref[...].reshape(sources * ROWS, HD).astype(jnp.float32)
     columns = []
     for quarter in range(2 * PIECE):
@@ -104,7 +110,7 @@
         ]
         columns.append(jnp.concatenate(column, axis=0).astype(jnp.bfloat16))
     columns = jnp.concatenate(columns, axis=1)
-    for step in range(WIDE // PICK_REQUESTS):
+    for step in range(PICK_STEPS):
         first = step * PICK_REQUESTS
         picked = jnp.dot(
             chosen_ref[first * MAXP : (first + PICK_REQUESTS) * MAXP],
@@ -113,9 +119,12 @@
         ).astype(jnp.bfloat16)
         for request in range(PICK_REQUESTS):
             for quarter in range(2 * PIECE):
-                out_ref[first + request, quarter * MAXP : (quarter + 1) * MAXP] = picked[
+                ready[first + request, quarter * MAXP : (quarter + 1) * MAXP] = picked[
                     request * MAXP : (request + 1) * MAXP, quarter * HD : (quarter + 1) * HD
                 ]
+        leave(step).start()
+    for step in range(PICK_STEPS):
+        leave(step).wait()
 
 
 def pick_pages(chosen, held):
@@ -124,14 +133,18 @@
         pick_kernel,
         out_shape=jax.ShapeDtypeStruct(shape, jnp.bfloat16),
         in_specs=[VMEM, VMEM],
-        out_specs=VMEM,
-        scratch_shapes=[pltpu.VMEM((held.shape[0] * 2 * ROWS, HD), jnp.float32)],
+        out_specs=HBM,
+        scratch_shapes=[
+            pltpu.VMEM((held.shape[0] * 2 * ROWS, HD), jnp.float32),
+            pltpu.VMEM(shape, jnp.bfloat16),
+            pltpu.SemaphoreType.DMA((PICK_STEPS,)),
+        ],
         compiler_params=PARAMS,
         name="pick_pages",
     )(chosen, held)
 
 
-HEADS_PER_STEP = 4
+HEADS_PER_STEP = 8
 CHUNK_WIDE = 8
 
 
@@ -141,76 +154,89 @@
     )
 
 
-def attend_kernel(length_ref, query_ref, key_ref, value_ref, held_ref, out_ref):
-    tokens = query_ref.shape[0]
+def attend_kernel(
+    query_ref, key_ref, value_ref, held_ref, seen_ref, out_hbm, keys_ref, values_ref, mixed_ref, sems
+):
+    tokens = key_ref.shape[0]
     group = query_ref.shape[1] // HD
     rows = HEADS_PER_STEP * tokens
+    width = HEADS_PER_STEP * HD
     half = PIECE * MAXP
-    keys = CHUNK_WIDE * half
+    count = CHUNK_WIDE * half
     chunks = WIDE // CHUNK_WIDE
-    length = length_ref[0]
-    at = lax.broadcasted_iota(jnp.int32, (1, keys), 1)
-    position = at % MAXP * PAGE + at // MAXP
-    biases = [
-        jnp.where(position + chunk * CHUNK_WIDE * PIECE < length, 0.0, HIDDEN)
-        for chunk in range(chunks)
-    ]
+    steps = group // HEADS_PER_STEP
+
+    def leave(step):
+        columns = pl.ds(step * width, width)
+        return pltpu.make_async_copy(mixed_ref.at[step], out_hbm.at[:, columns], sems.at[step])
+
+    first_key = held_ref[0, 0:1, :]
+    for chunk in range(chunks):
+        wide = slice(chunk * CHUNK_WIDE, (chunk + 1) * CHUNK_WIDE)
+        at = slice(chunk * count, (chunk + 1) * count)
+        seen = seen_ref[at]
+        visible = seen > 0
+        keys_ref[at] = jnp.where(visible, held_ref[wide, :half].reshape(count, HD), first_key)
+        values = held_ref[wide, half:].reshape(count, HD)
+        values_ref[at, :HD] = jnp.where(visible, values, jnp.zeros_like(values))
+        values_ref[at, HD:] = seen
+    fresh_values = jnp.concatenate(
+        [value_ref[...], jnp.ones((tokens, HD), jnp.bfloat16)], axis=1
+    )
     token = lax.broadcasted_iota(jnp.int32, (rows, tokens), 0) % tokens
     causal = lax.broadcasted_iota(jnp.int32, (rows, tokens), 1) <= token
-
-    def held(chunk, kind):
-        block = held_ref[
-            chunk * CHUNK_WIDE : (chunk + 1) * CHUNK_WIDE, kind * half : (kind + 1) * half
-        ]
-        return block.reshape(keys, HD)
-
-    for step in range(group // HEADS_PER_STEP):
-        first = step * HEADS_PER_STEP
+    for step in range(steps):
         query = jnp.concatenate(
             [
-                query_ref[:, (first + n) * HD : (first + n + 1) * HD]
-                for n in range(HEADS_PER_STEP)
+                query_ref[:, head * HD : (head + 1) * HD]
+                for head in range(step * HEADS_PER_STEP, (step + 1) * HEADS_PER_STEP)
             ],
             axis=0,
         )
         fresh = jnp.where(causal, contract_last(query, key_ref[...]), HIDDEN)
         scores = [
-            contract_last(query, held(chunk, 0)) + biases[chunk] for chunk in range(chunks)
+            contract_last(query, keys_ref[chunk * count : (chunk + 1) * count])
+            for chunk in range(chunks)
         ]
         top = functools.reduce(jnp.maximum, scores)
         highest = jnp.maximum(
             jnp.max(top, axis=1, keepdims=True), jnp.max(fresh, axis=1, keepdims=True)
         )
-        fresh = jnp.exp2((fresh - highest) * EXP2_SCALE)
         mixed = jnp.dot(
-            fresh.astype(jnp.bfloat16), value_ref[...], preferred_element_type=jnp.float32
-        )
-        total = None
-        for chunk in range(chunks):
-            weights = jnp.exp2((scores[chunk] - highest) * EXP2_SCALE)
-            total = weights if total is None else total + weights
-            mixed += jnp.dot(
-                weights.astype(jnp.bfloat16), held(chunk, 1), preferred_element_type=jnp.float32
-            )
-        weight_sum = jnp.sum(total, axis=1, keepdims=True) + jnp.sum(
-            fresh, axis=1, keepdims=True
-        )
-        mixed = (mixed / weight_sum).astype(jnp.bfloat16)
+            jnp.exp2((fresh - highest) * EXP2_SCALE).astype(jnp.bfloat16),
+            fresh_values,
+            preferred_element_type=jnp.float32,
+        )
+        weights = [jnp.exp2((part - highest) * EXP2_SCALE).astype(jnp.bfloat16) for part in scores]
+        mixed += jnp.dot(
+            jnp.concatenate(weights, axis=1), values_ref[...], preferred_element_type=jnp.float32
+        )
+        mixed = (mixed[:, :HD] / mixed[:, HD:]).astype(jnp.bfloat16)
         for n in range(HEADS_PER_STEP):
-            out_ref[:, (first + n) * HD : (first + n + 1) * HD] = mixed[
-                n * tokens : (n + 1) * tokens
-            ]
-
-
-def attend(length, query, key_new, value_new, held):
+            mixed_ref[step, :, n * HD : (n + 1) * HD] = mixed[n * tokens : (n + 1) * tokens]
+        leave(step).start()
+    for step in range(steps):
+        leave(step).wait()
+
+
+def attend(query, key_new, value_new, held, seen):
+    tokens, width = query.shape
+    keys = WIDE * PIECE * MAXP
+    steps = width // HD // HEADS_PER_STEP
     return pl.pallas_call(
         attend_kernel,
-        out_shape=jax.ShapeDtypeStruct(query.shape, jnp.bfloat16),
-        in_specs=[SMEM, VMEM, VMEM, VMEM, VMEM],
-        out_specs=VMEM,
+        out_shape=jax.ShapeDtypeStruct((tokens, width), jnp.bfloat16),
+        in_specs=[VMEM] * 5,
+        out_specs=HBM,
+        scratch_shapes=[
+            pltpu.VMEM((keys, HD), jnp.bfloat16),
+            pltpu.VMEM((keys, 2 * HD), jnp.bfloat16),
+            pltpu.VMEM((steps, tokens, HEADS_PER_STEP * HD), jnp.bfloat16),
+            pltpu.SemaphoreType.DMA((steps,)),
+        ],
         compiler_params=PARAMS,
         name="attend",
-    )(length, query, key_new, value_new, held)
+    )(query, key_new, value_new, held, seen)
 
 
 def exchange(array, axes):
@@ -219,7 +245,10 @@
 
 def body(query, key_new, value_new, key_cache, value_cache, page_table, prefix_len):
     own_request = lax.axis_index(WIDE_AXES)
-    length = lax.dynamic_slice_in_dim(prefix_len, own_request, 1)
+    length = jnp.take(prefix_len, own_request)
+    at = jnp.arange(WIDE * PIECE * MAXP, dtype=jnp.int32)
+    seen = at % MAXP * PAGE + at // MAXP < length
+    seen = jnp.broadcast_to(seen[:, None], (at.shape[0], HD)).astype(jnp.bfloat16)
     sources = WIDE * HEADS
     pages = page_table.reshape(-1)
     column = pages % STORED * sources + pages // STORED
@@ -229,7 +258,7 @@
     pieces = exchange(pieces, WIDE_AXES + HEAD_AXES)
     picked = pick_pages(chosen, pieces.reshape(sources // 2, 2 * ROWS, HD))
     held = exchange(picked, WIDE_AXES)
-    return attend(length, query, key_new, value_new, held)
+    return attend(query, key_new, value_new, held, seen)
 
 
 def solution(mesh):

time: 102 us -> 98.2 us (0.963)
  Pallas kernels: 10.1 us -> 8.29 us
  local copies, waits for them, and re-layouts: 2.87 us -> 1.12 us
    unnamed x15 -> x11, local copies, waits for them, and re-layouts: 2.18 us -> 0.11 us
    pallas_call x1, Pallas kernels: 5.18 us -> 3.54 us  [attend(): pl.pallas_call(attend_kernel, out_shape=jax.ShapeDtypeStruct((tokens, wid...]
where the time goes in v3:
time: 98.2 us; the launch traced here: 97.3 us
  waiting for transfers between devices  58.8 us (60%)
  starting transfers between devices  27.8 us (28%)
  Pallas kernels  8.29 us (8%)
  local copies, waits for them, and re-layouts  1.12 us (1%)
    all_to_all x2, waiting for transfers between devices, exchange(): return lax.all_to_all(array, axes, split_axis=0, concat_axis=0, tiled=True)  58.8 us
    all_to_all x2, starting transfers between devices, exchange(): return lax.all_to_all(array, axes, split_axis=0, concat_axis=0, tiled=True)  27.8 us
    pallas_call x1, Pallas kernels, attend(): pl.pallas_call(attend_kernel, out_shape=jax.ShapeDtypeStruct((tokens, wid...  3.54 us
    pallas_call x1, Pallas kernels, split_pages(): pl.pallas_call(split_kernel, out_shape=jax.ShapeDtypeStruct(shape, jnp.bf...  2.5 us
    pallas_call x1, Pallas kernels, pick_pages(): pl.pallas_call(pick_kernel, out_shape=jax.ShapeDtypeStruct(shape, jnp.bfl...  2.25 us
  transfers between devices with their start and end apart: 2, of which 2 were waited for; matrix products, arithmetic and copies ran while one was open for 1% of the time, Pallas kernels for 0%

profile of v3, /device:TPU:1, one launch (start us, length us, event | category | flops | bytes accessed | tf_op | source)
XLA Modules:
  0.0 97.3 jit_solution(10529152051421786233)
XLA Ops:
  0.0 0.0 copy-start.3
  0.0 2.5 %split_pages.1 = bf16[64,4,16,128]{3,2,1,0:T(8,128)(2,1)} custom-call(bf16[2,128,1024]{2,1,0:T(8,128)(2,1)} %key_hbm.1, bf16[2,128,1024]{2,1,0:T(8,128)(2,1)} %value_hbm.1), custom_call_target="tpu_custom_call" | custom-call | tf_op jit(solution)/shard_map/split_pages/pallas_call | solution.py:77
  2.5 22.2 %all-to-all-start = ((bf16[512,8,128]{2,1,0:T(8,128)(2,1)}), bf16[512,8,128]{2,1,0:T(8,128)(2,1)S(1)}, u32[]{:S(2)}, u32[]{:S(2)}) async-start(bf16[512,8,128]{2,1,0:T(8,128)(2,1)} %bitcast.5), calls=%async_computation | async-start | bytes 2097152 | tf_op jit(solution)/shard_map/all_to_all | solution.py:243
  24.7 0.0 copy-done.3
  24.7 0.1 copy.8
  24.8 0.1 reshape.83
  24.9 0.4 fusion.chosen_ref
  25.3 31.8 %all-to-all-done = bf16[512,8,128]{2,1,0:T(8,128)(2,1)S(1)} async-done(((bf16[512,8,128]{2,1,0:T(8,128)(2,1)}), bf16[512,8,128]{2,1,0:T(8,128)(2,1)S(1)}, u32[]{:S(2)}, u32[]{:S(2)}) %all-to-all-start) | async-done | bytes 1048608 | tf_op jit(solution)/shard_map/all_to_all | solution.py:243
  57.1 2.2 %pick_pages.1 = bf16[64,64,128]{2,1,0:T(8,128)(2,1)} custom-call(bf16[1024,1024]{1,0:T(8,128)(2,1)S(1)} %fusion.chosen_ref, bf16[256,16,128]{2,1,0:T(8,128)(2,1)S(1)} %bitcast.4), custom_call_target="tpu_custom_call" | custom-call | tf_op jit(solution)/shard_map/pick_pages/pallas_call | solution.py:132
  59.4 0.0 copy-start.4
  59.4 0.0 copy-start
  59.4 0.0 copy-start.1
  59.4 0.0 copy-start.2
  59.4 5.7 %all-to-all-start.1 = ((bf16[64,64,128]{2,1,0:T(8,128)(2,1)}), bf16[64,64,128]{2,1,0:T(8,128)(2,1)S(1)}, u32[]{:S(2)}, u32[]{:S(2)}) async-start(bf16[64,64,128]{2,1,0:T(8,128)(2,1)} %pick_pages.1), calls=%async_computation.1 | async-start | bytes 2097152 | tf_op jit(solution)/shard_map/all_to_all | solution.py:243
  65.1 0.0 copy-done.4
  65.1 0.6 dynamic-slice.2
  66.4 27.0 %all-to-all-done.1.held_ref = bf16[64,64,128]{2,1,0:T(8,128)(2,1)S(1)} async-done(((bf16[64,64,128]{2,1,0:T(8,128)(2,1)}), bf16[64,64,128]{2,1,0:T(8,128)(2,1)S(1)}, u32[]{:S(2)}, u32[]{:S(2)}) %all-to-all-start.1) | async-done | bytes 1048608 | tf_op jit(solution)/shard_map/all_to_all | solution.py:243
  93.4 0.3 broadcast_in_dim.7.seen_ref
  93.7 0.0 copy-done
  93.7 0.0 copy-done.1
  93.7 0.0 copy-done.2
  93.7 3.5 %attend.1 = bf16[64,2048]{1,0:T(8,128)(2,1)} custom-call(bf16[64,2048]{1,0:T(8,128)(2,1)S(1)} %copy-done, bf16[64,128]{1,0:T(8,128)(2,1)S(1)} %copy-done.1, bf16[64,128]{1,0:T(8,128)(2,1)S(1)} %copy-done.2, bf16[64,64,128]{2,1,0:T(8,128)(2,1)S(1)} %all-to-all-done.1.held_ref, bf16[2048,128]{1,0:T(8,128)(2,1)S(1)} %broadcast_in_dim.7.seen_ref), custom_call_target="tpu_custom_call" | custom-call | tf_op jit(solution)/shard_map/attend/pallas_call | solution.py:226
  (2 shorter events, 0.0 us)
Async XLA Ops:
  0.0 24.7 %copy-start.3 = (s32[64,16]{0,1:T(8,128)S(1)}, s32[64,16]{0,1:T(8,128)}, u32[]{:S(2)}) copy-start(s32[64,16]{0,1:T(8,128)} %param.12) | copy-start | bytes 12292
  2.5 54.6 %all-to-all-start = ((bf16[512,8,128]{2,1,0:T(8,128)(2,1)}), bf16[512,8,128]{2,1,0:T(8,128)(2,1)S(1)}, u32[]{:S(2)}, u32[]{:S(2)}) async-start(bf16[512,8,128]{2,1,0:T(8,128)(2,1)} %bitcast.5), calls=%async_computation | async-start | bytes 2097152 | tf_op jit(solution)/shard_map/all_to_all | solution.py:243
  59.4 5.7 %copy-start.4 = (s32[64]{0:T(128)S(1)}, s32[64]{0:T(128)}, u32[]{:S(2)}) copy-start(s32[64]{0:T(128)} %param.13) | copy-start | bytes 772
  59.4 34.3 %copy-start = (bf16[64,2048]{1,0:T(8,128)(2,1)S(1)}, bf16[64,2048]{1,0:T(8,128)(2,1)}, u32[]{:S(2)}) copy-start(bf16[64,2048]{1,0:T(8,128)(2,1)} %query_ref.1) | copy-start | bytes 786436
  59.4 34.3 %copy-start.1 = (bf16[64,128]{1,0:T(8,128)(2,1)S(1)}, bf16[64,128]{1,0:T(8,128)(2,1)}, u32[]{:S(2)}) copy-start(bf16[64,128]{1,0:T(8,128)(2,1)} %key_ref.1) | copy-start | bytes 49156
  59.4 34.3 %copy-start.2 = (bf16[64,128]{1,0:T(8,128)(2,1)S(1)}, bf16[64,128]{1,0:T(8,128)(2,1)}, u32[]{:S(2)}) copy-start(bf16[64,128]{1,0:T(8,128)(2,1)} %value_ref.1) | copy-start | bytes 49156
  59.4 34.0 %all-to-all-start.1 = ((bf16[64,64,128]{2,1,0:T(8,128)(2,1)}), bf16[64,64,128]{2,1,0:T(8,128)(2,1)S(1)}, u32[]{:S(2)}, u32[]{:S(2)}) async-start(bf16[64,64,128]{2,1,0:T(8,128)(2,1)} %pick_pages.1), calls=%async_computation.1 | async-start | bytes 2097152 | tf_op jit(solution)/shard_map/all_to_all | solution.py:243

commit v4 on v3

--- a/solution.py
+++ b/solution.py
@@ -25,6 +25,7 @@
 ALL_PARAMS = pltpu.CompilerParams(vmem_limit_bytes=63 * 2**20)
 VMEM = pl.BlockSpec(memory_space=pltpu.VMEM)
 HBM = pl.BlockSpec(memory_space=pltpu.HBM)
+ANY = pl.BlockSpec(memory_space=pl.ANY)
 
 PARTS = 2
 PART_TOKENS = PAGE // PARTS
@@ -94,7 +95,8 @@
 PICK_STEPS = WIDE // PICK_REQUESTS
 
 
-def pick_kernel(chosen_ref, held_ref, out_hbm, spread, ready, sems):
+def pick_kernel(chosen_ref, held_ref, seen_any, out_hbm, spread, ready, sems):
+    del seen_any
     sources = held_ref.shape[0] * 2
 
     def leave(step):
@@ -127,12 +129,12 @@
         leave(step).wait()
 
 
-def pick_pages(chosen, held):
+def pick_pages(chosen, held, seen):
     shape = (WIDE, 2 * PIECE * MAXP, HD)
     return pl.pallas_call(
         pick_kernel,
         out_shape=jax.ShapeDtypeStruct(shape, jnp.bfloat16),
-        in_specs=[VMEM, VMEM],
+        in_specs=[VMEM, VMEM, ANY],
         out_specs=HBM,
         scratch_shapes=[
             pltpu.VMEM((held.shape[0] * 2 * ROWS, HD), jnp.float32),
@@ -141,7 +143,7 @@
         ],
         compiler_params=PARAMS,
         name="pick_pages",
-    )(chosen, held)
+    )(chosen, held, seen)
 
 
 HEADS_PER_STEP = 8
@@ -256,7 +258,7 @@
     chosen = (column[:, None] == every[None, :]).astype(jnp.bfloat16)
     pieces = split_pages(key_cache, value_cache).reshape(sources, ROWS, HD)
     pieces = exchange(pieces, WIDE_AXES + HEAD_AXES)
-    picked = pick_pages(chosen, pieces.reshape(sources // 2, 2 * ROWS, HD))
+    picked = pick_pages(chosen, pieces.reshape(sources // 2, 2 * ROWS, HD), seen)
     held = exchange(picked, WIDE_AXES)
     return attend(query, key_new, value_new, held, seen)
 

time: 98.2 us -> 97.3 us (level)
  blocking collectives: 0 us -> 33.7 us
  waiting for transfers between devices: 58.8 us -> 30.5 us
  starting transfers between devices: 27.8 us -> 22.2 us
    all_to_all x0 -> x1, blocking collectives: none -> 33.7 us  [exchange(): return lax.all_to_all(array, axes, split_axis=0, concat_axis=0, tiled=True)]
    all_to_all x2 -> x1, waiting for transfers between devices: 58.8 us -> 30.5 us  [exchange(): return lax.all_to_all(array, axes, split_axis=0, concat_axis=0, tiled=True)]
    all_to_all x2 -> x1, starting transfers between devices: 27.8 us -> 22.2 us  [exchange(): return lax.all_to_all(array, axes, split_axis=0, concat_axis=0, tiled=True)]
  transfers between devices with their start and end apart: 2 -> 1, of which waited for: 2 -> 1; matrix products, arithmetic and copies ran while one was open for 1% -> 1% of each run, Pallas kernels for 0% -> 0%
where the time goes in v4:
time: 97.3 us; the launch traced here: 96.5 us
  blocking collectives  33.7 us (35%)
  waiting for transfers between devices  30.5 us (31%)
  starting transfers between devices  22.2 us (23%)
  Pallas kernels  7.75 us (8%)
  local copies, waits for them, and re-layouts  1.13 us (1%)
    all_to_all x1, blocking collectives, exchange(): return lax.all_to_all(array, axes, split_axis=0, concat_axis=0, tiled=True)  33.7 us
    all_to_all x1, waiting for transfers between devices, exchange(): return lax.all_to_all(array, axes, split_axis=0, concat_axis=0, tiled=True)  30.5 us
    all_to_all x1, starting transfers between devices, exchange(): return lax.all_to_all(array, axes, split_axis=0, concat_axis=0, tiled=True)  22.2 us
    pallas_call x1, Pallas kernels, attend(): pl.pallas_call(attend_kernel, out_shape=jax.ShapeDtypeStruct((tokens, wid...  3.54 us
    pallas_call x1, Pallas kernels, split_pages(): pl.pallas_call(split_kernel, out_shape=jax.ShapeDtypeStruct(shape, jnp.bf...  2.51 us
  transfers between devices with their start and end apart: 1, of which 1 were waited for; matrix products, arithmetic and copies ran while one was open for 1% of the time, Pallas kernels for 0%

profile of v4, /device:TPU:1, one launch (start us, length us, event | category | flops | bytes accessed | tf_op | source)
XLA Modules:
  0.0 96.5 jit_solution(5929188890057830612)
XLA Ops:
  0.0 0.0 copy-start.4
  0.0 0.0 copy-start.3
  0.0 2.5 %split_pages.1 = bf16[64,4,16,128]{3,2,1,0:T(8,128)(2,1)} custom-call(bf16[2,128,1024]{2,1,0:T(8,128)(2,1)} %key_hbm.1, bf16[2,128,1024]{2,1,0:T(8,128)(2,1)} %value_hbm.1), custom_call_target="tpu_custom_call" | custom-call | tf_op jit(solution)/shard_map/split_pages/pallas_call | solution.py:78
  2.5 22.2 %all-to-all-start = ((bf16[512,8,128]{2,1,0:T(8,128)(2,1)}), bf16[512,8,128]{2,1,0:T(8,128)(2,1)S(1)}, u32[]{:S(2)}, u32[]{:S(2)}) async-start(bf16[512,8,128]{2,1,0:T(8,128)(2,1)} %bitcast.5), calls=%async_computation | async-start | bytes 2097152 | tf_op jit(solution)/shard_map/all_to_all | solution.py:245
  24.7 0.0 copy-done.4
  24.7 0.6 dynamic-slice.2
  25.3 0.0 copy-done.3
  25.3 0.1 copy.8
  25.4 0.1 reshape.83
  26.2 0.4 fusion.chosen_ref
  26.6 30.5 %all-to-all-done = bf16[512,8,128]{2,1,0:T(8,128)(2,1)S(1)} async-done(((bf16[512,8,128]{2,1,0:T(8,128)(2,1)}), bf16[512,8,128]{2,1,0:T(8,128)(2,1)S(1)}, u32[]{:S(2)}, u32[]{:S(2)}) %all-to-all-start) | async-done | bytes 1048608 | tf_op jit(solution)/shard_map/all_to_all | solution.py:245
  57.1 0.3 broadcast_in_dim.7.seen_any.seen_ref
  57.5 1.7 %pick_pages.1 = bf16[64,64,128]{2,1,0:T(8,128)(2,1)S(1)} custom-call(bf16[1024,1024]{1,0:T(8,128)(2,1)S(1)} %fusion.chosen_ref, bf16[256,16,128]{2,1,0:T(8,128)(2,1)S(1)} %bitcast.4, bf16[2048,128]{1,0:T(8,128)(2,1)S(1)} %broadcast_in_dim.7.seen_any.seen_ref), custom_call_target="tpu_custom_call" | custom-call | tf_op jit(solution)/shard_map/pick_pages/pallas_call | solution.py:134
  59.1 0.0 copy-start
  59.2 0.0 copy-start.1
  59.2 0.0 copy-start.2
  59.2 33.7 %all_to_all.10.held_ref = bf16[64,64,128]{2,1,0:T(8,128)(2,1)S(1)} all-to-all(bf16[64,64,128]{2,1,0:T(8,128)(2,1)S(1)} %pick_pages.1), channel_id=1, replica_groups=mesh['y_lo'=2,'x'=4,'z'=8,'y_hi'=4,'core'=2] {'y_lo','x','z'}, dimensions={0} | all-to-all | bytes 2097152 | tf_op jit(solution)/shard_map/all_to_all | solution.py:245
  92.9 0.0 copy-done
  92.9 0.0 copy-done.1
  92.9 0.0 copy-done.2
  92.9 3.5 %attend.1 = bf16[64,2048]{1,0:T(8,128)(2,1)} custom-call(bf16[64,2048]{1,0:T(8,128)(2,1)S(1)} %copy-done, bf16[64,128]{1,0:T(8,128)(2,1)S(1)} %copy-done.1, bf16[64,128]{1,0:T(8,128)(2,1)S(1)} %copy-done.2, bf16[64,64,128]{2,1,0:T(8,128)(2,1)S(1)} %all_to_all.10.held_ref, bf16[2048,128]{1,0:T(8,128)(2,1)S(1)} %broadcast_in_dim.7.seen_any.seen_ref), custom_call_target="tpu_custom_call" | custom-call | tf_op jit(solution)/shard_map/attend/pallas_call | solution.py:228
  (2 shorter events, 0.0 us)
Async XLA Ops:
  0.0 24.7 %copy-start.4 = (s32[64]{0:T(128)S(1)}, s32[64]{0:T(128)}, u32[]{:S(2)}) copy-start(s32[64]{0:T(128)} %param.13) | copy-start | bytes 772
  0.0 25.3 %copy-start.3 = (s32[64,16]{0,1:T(8,128)S(1)}, s32[64,16]{0,1:T(8,128)}, u32[]{:S(2)}) copy-start(s32[64,16]{0,1:T(8,128)} %param.12) | copy-start | bytes 12292
  2.5 54.6 %all-to-all-start = ((bf16[512,8,128]{2,1,0:T(8,128)(2,1)}), bf16[512,8,128]{2,1,0:T(8,128)(2,1)S(1)}, u32[]{:S(2)}, u32[]{:S(2)}) async-start(bf16[512,8,128]{2,1,0:T(8,128)(2,1)} %bitcast.5), calls=%async_computation | async-start | bytes 2097152 | tf_op jit(solution)/shard_map/all_to_all | solution.py:245
  59.1 33.8 %copy-start = (bf16[64,2048]{1,0:T(8,128)(2,1)S(1)}, bf16[64,2048]{1,0:T(8,128)(2,1)}, u32[]{:S(2)}) copy-start(bf16[64,2048]{1,0:T(8,128)(2,1)} %query_ref.1) | copy-start | bytes 786436
  59.2 33.8 %copy-start.1 = (bf16[64,128]{1,0:T(8,128)(2,1)S(1)}, bf16[64,128]{1,0:T(8,128)(2,1)}, u32[]{:S(2)}) copy-start(bf16[64,128]{1,0:T(8,128)(2,1)} %key_ref.1) | copy-start | bytes 49156
  59.2 33.8 %copy-start.2 = (bf16[64,128]{1,0:T(8,128)(2,1)S(1)}, bf16[64,128]{1,0:T(8,128)(2,1)}, u32[]{:S(2)}) copy-start(bf16[64,128]{1,0:T(8,128)(2,1)} %value_ref.1) | copy-start | bytes 49156

commit v5 on v4

--- a/solution.py
+++ b/solution.py
@@ -172,7 +172,7 @@
         columns = pl.ds(step * width, width)
         return pltpu.make_async_copy(mixed_ref.at[step], out_hbm.at[:, columns], sems.at[step])
 
-    first_key = held_ref[0, 0:1, :]
+    first_key = held_ref[0, :MAXP][:1]
     for chunk in range(chunks):
         wide = slice(chunk * CHUNK_WIDE, (chunk + 1) * CHUNK_WIDE)
         at = slice(chunk * count, (chunk + 1) * count)

time: 97.3 us -> 97.3 us (level)
  no operation moved by 1% of the time
where the time goes in v5:
time: 97.3 us; the launch traced here: 96.5 us
  blocking collectives  33.7 us (35%)
  waiting for transfers between devices  30.5 us (31%)
  starting transfers between devices  22.2 us (23%)
  Pallas kernels  7.74 us (8%)
  local copies, waits for them, and re-layouts  1.13 us (1%)
    all_to_all x1, blocking collectives, exchange(): return lax.all_to_all(array, axes, split_axis=0, concat_axis=0, tiled=True)  33.7 us
    all_to_all x1, waiting for transfers between devices, exchange(): return lax.all_to_all(array, axes, split_axis=0, concat_axis=0, tiled=True)  30.5 us
    all_to_all x1, starting transfers between devices, exchange(): return lax.all_to_all(array, axes, split_axis=0, concat_axis=0, tiled=True)  22.2 us
    pallas_call x1, Pallas kernels, attend(): pl.pallas_call(attend_kernel, out_shape=jax.ShapeDtypeStruct((tokens, wid...  3.54 us
    pallas_call x1, Pallas kernels, split_pages(): pl.pallas_call(split_kernel, out_shape=jax.ShapeDtypeStruct(shape, jnp.bf...  2.51 us
  transfers between devices with their start and end apart: 1, of which 1 were waited for; matrix products, arithmetic and copies ran while one was open for 1% of the time, Pallas kernels for 0%

profile of v5, /device:TPU:1, one launch (start us, length us, event | category | flops | bytes accessed | tf_op | source)
XLA Modules:
  0.0 96.5 jit_solution(3653370350112265797)
XLA Ops:
  0.0 0.0 copy-start.4
  0.0 0.0 copy-start.3
  0.0 2.5 %split_pages.1 = bf16[64,4,16,128]{3,2,1,0:T(8,128)(2,1)} custom-call(bf16[2,128,1024]{2,1,0:T(8,128)(2,1)} %key_hbm.1, bf16[2,128,1024]{2,1,0:T(8,128)(2,1)} %value_hbm.1), custom_call_target="tpu_custom_call" | custom-call | tf_op jit(solution)/shard_map/split_pages/pallas_call | solution.py:78
  2.5 22.2 %all-to-all-start = ((bf16[512,8,128]{2,1,0:T(8,128)(2,1)}), bf16[512,8,128]{2,1,0:T(8,128)(2,1)S(1)}, u32[]{:S(2)}, u32[]{:S(2)}) async-start(bf16[512,8,128]{2,1,0:T(8,128)(2,1)} %bitcast.5), calls=%async_computation | async-start | bytes 2097152 | tf_op jit(solution)/shard_map/all_to_all | solution.py:245
  24.7 0.0 copy-done.4
  24.7 0.6 dynamic-slice.2
  25.3 0.0 copy-done.3
  25.3 0.1 copy.8
  25.4 0.1 reshape.83
  26.2 0.4 fusion.chosen_ref
  26.6 30.5 %all-to-all-done = bf16[512,8,128]{2,1,0:T(8,128)(2,1)S(1)} async-done(((bf16[512,8,128]{2,1,0:T(8,128)(2,1)}), bf16[512,8,128]{2,1,0:T(8,128)(2,1)S(1)}, u32[]{:S(2)}, u32[]{:S(2)}) %all-to-all-start) | async-done | bytes 1048608 | tf_op jit(solution)/shard_map/all_to_all | solution.py:245
  57.1 0.3 broadcast_in_dim.7.seen_any.seen_ref
  57.5 1.7 %pick_pages.1 = bf16[64,64,128]{2,1,0:T(8,128)(2,1)S(1)} custom-call(bf16[1024,1024]{1,0:T(8,128)(2,1)S(1)} %fusion.chosen_ref, bf16[256,16,128]{2,1,0:T(8,128)(2,1)S(1)} %bitcast.4, bf16[2048,128]{1,0:T(8,128)(2,1)S(1)} %broadcast_in_dim.7.seen_any.seen_ref), custom_call_target="tpu_custom_call" | custom-call | tf_op jit(solution)/shard_map/pick_pages/pallas_call | solution.py:134
  59.1 0.0 copy-start
  59.2 0.0 copy-start.1
  59.2 0.0 copy-start.2
  59.2 33.7 %all_to_all.10.held_ref = bf16[64,64,128]{2,1,0:T(8,128)(2,1)S(1)} all-to-all(bf16[64,64,128]{2,1,0:T(8,128)(2,1)S(1)} %pick_pages.1), channel_id=1, replica_groups=mesh['y_lo'=2,'x'=4,'z'=8,'y_hi'=4,'core'=2] {'y_lo','x','z'}, dimensions={0} | all-to-all | bytes 2097152 | tf_op jit(solution)/shard_map/all_to_all | solution.py:245
  92.9 0.0 copy-done
  92.9 0.0 copy-done.1
  92.9 0.0 copy-done.2
  92.9 3.5 %attend.1 = bf16[64,2048]{1,0:T(8,128)(2,1)} custom-call(bf16[64,2048]{1,0:T(8,128)(2,1)S(1)} %copy-done, bf16[64,128]{1,0:T(8,128)(2,1)S(1)} %copy-done.1, bf16[64,128]{1,0:T(8,128)(2,1)S(1)} %copy-done.2, bf16[64,64,128]{2,1,0:T(8,128)(2,1)S(1)} %all_to_all.10.held_ref, bf16[2048,128]{1,0:T(8,128)(2,1)S(1)} %broadcast_in_dim.7.seen_any.seen_ref), custom_call_target="tpu_custom_call" | custom-call | tf_op jit(solution)/shard_map/attend/pallas_call | solution.py:228
  (2 shorter events, 0.0 us)
Async XLA Ops:
  0.0 24.7 %copy-start.4 = (s32[64]{0:T(128)S(1)}, s32[64]{0:T(128)}, u32[]{:S(2)}) copy-start(s32[64]{0:T(128)} %param.13) | copy-start | bytes 772
  0.0 25.3 %copy-start.3 = (s32[64,16]{0,1:T(8,128)S(1)}, s32[64,16]{0,1:T(8,128)}, u32[]{:S(2)}) copy-start(s32[64,16]{0,1:T(8,128)} %param.12) | copy-start | bytes 12292
  2.5 54.6 %all-to-all-start = ((bf16[512,8,128]{2,1,0:T(8,128)(2,1)}), bf16[512,8,128]{2,1,0:T(8,128)(2,1)S(1)}, u32[]{:S(2)}, u32[]{:S(2)}) async-start(bf16[512,8,128]{2,1,0:T(8,128)(2,1)} %bitcast.5), calls=%async_computation | async-start | bytes 2097152 | tf_op jit(solution)/shard_map/all_to_all | solution.py:245
  59.1 33.8 %copy-start = (bf16[64,2048]{1,0:T(8,128)(2,1)S(1)}, bf16[64,2048]{1,0:T(8,128)(2,1)}, u32[]{:S(2)}) copy-start(bf16[64,2048]{1,0:T(8,128)(2,1)} %query_ref.1) | copy-start | bytes 786436
  59.2 33.8 %copy-start.1 = (bf16[64,128]{1,0:T(8,128)(2,1)S(1)}, bf16[64,128]{1,0:T(8,128)(2,1)}, u32[]{:S(2)}) copy-start(bf16[64,128]{1,0:T(8,128)(2,1)} %key_ref.1) | copy-start | bytes 49156
  59.2 33.8 %copy-start.2 = (bf16[64,128]{1,0:T(8,128)(2,1)S(1)}, bf16[64,128]{1,0:T(8,128)(2,1)}, u32[]{:S(2)}) copy-start(bf16[64,128]{1,0:T(8,128)(2,1)} %value_ref.1) | copy-start | bytes 49156

commit v6 on v5

--- a/solution.py
+++ b/solution.py
@@ -95,14 +95,9 @@
 PICK_STEPS = WIDE // PICK_REQUESTS
 
 
-def pick_kernel(chosen_ref, held_ref, seen_any, out_hbm, spread, ready, sems):
+def pick_kernel(chosen_ref, held_ref, seen_any, ready, spread):
     del seen_any
     sources = held_ref.shape[0] * 2
-
-    def leave(step):
-        requests = pl.ds(step * PICK_REQUESTS, PICK_REQUESTS)
-        return pltpu.make_async_copy(ready.at[requests], out_hbm.at[requests], sems.at[step])
-
     spread[...] = held_ref[...].reshape(sources * ROWS, HD).astype(jnp.float32)
     columns = []
     for quarter in range(2 * PIECE):
@@ -124,9 +119,6 @@
                 ready[first + request, quarter * MAXP : (quarter + 1) * MAXP] = picked[
                     request * MAXP : (request + 1) * MAXP, quarter * HD : (quarter + 1) * HD
                 ]
-        leave(step).start()
-    for step in range(PICK_STEPS):
-        leave(step).wait()
 
 
 def pick_pages(chosen, held, seen):
@@ -135,11 +127,9 @@
         pick_kernel,
         out_shape=jax.ShapeDtypeStruct(shape, jnp.bfloat16),
         in_specs=[VMEM, VMEM, ANY],
-        out_specs=HBM,
+        out_specs=VMEM,
         scratch_shapes=[
             pltpu.VMEM((held.shape[0] * 2 * ROWS, HD), jnp.float32),
-            pltpu.VMEM(shape, jnp.bfloat16),
-            pltpu.SemaphoreType.DMA((PICK_STEPS,)),
         ],
         compiler_params=PARAMS,
         name="pick_pages",

time: 97.3 us -> 97.1 us (level)
  no operation moved by 1% of the time
where the time goes in v6:
time: 97.1 us; the launch traced here: 96.2 us
  blocking collectives  33.7 us (35%)
  waiting for transfers between devices  30.5 us (31%)
  starting transfers between devices  22.2 us (23%)
  Pallas kernels  7.48 us (8%)
  local copies, waits for them, and re-layouts  1.13 us (1%)
    all_to_all x1, blocking collectives, exchange(): return lax.all_to_all(array, axes, split_axis=0, concat_axis=0, tiled=True)  33.7 us
    all_to_all x1, waiting for transfers between devices, exchange(): return lax.all_to_all(array, axes, split_axis=0, concat_axis=0, tiled=True)  30.5 us
    all_to_all x1, starting transfers between devices, exchange(): return lax.all_to_all(array, axes, split_axis=0, concat_axis=0, tiled=True)  22.2 us
    pallas_call x1, Pallas kernels, attend(): pl.pallas_call(attend_kernel, out_shape=jax.ShapeDtypeStruct((tokens, wid...  3.54 us
    pallas_call x1, Pallas kernels, split_pages(): pl.pallas_call(split_kernel, out_shape=jax.ShapeDtypeStruct(shape, jnp.bf...  2.51 us
  transfers between devices with their start and end apart: 1, of which 1 were waited for; matrix products, arithmetic and copies ran while one was open for 1% of the time, Pallas kernels for 0%

profile of v6, /device:TPU:1, one launch (start us, length us, event | category | flops | bytes accessed | tf_op | source)
XLA Modules:
  0.0 96.2 jit_solution(1744171413060717427)
XLA Ops:
  0.0 0.0 copy-start.4
  0.0 0.0 copy-start.3
  0.0 2.5 %split_pages.1 = bf16[64,4,16,128]{3,2,1,0:T(8,128)(2,1)} custom-call(bf16[2,128,1024]{2,1,0:T(8,128)(2,1)} %key_hbm.1, bf16[2,128,1024]{2,1,0:T(8,128)(2,1)} %value_hbm.1), custom_call_target="tpu_custom_call" | custom-call | tf_op jit(solution)/shard_map/split_pages/pallas_call | solution.py:78
  2.5 22.2 %all-to-all-start = ((bf16[512,8,128]{2,1,0:T(8,128)(2,1)}), bf16[512,8,128]{2,1,0:T(8,128)(2,1)S(1)}, u32[]{:S(2)}, u32[]{:S(2)}) async-start(bf16[512,8,128]{2,1,0:T(8,128)(2,1)} %bitcast.5), calls=%async_computation | async-start | bytes 2097152 | tf_op jit(solution)/shard_map/all_to_all | solution.py:235
  24.7 0.0 copy-done.4
  24.7 0.6 dynamic-slice.2
  25.3 0.0 copy-done.3
  25.3 0.1 copy.8
  25.4 0.1 reshape.83
  26.2 0.4 fusion.chosen_ref
  26.6 30.5 %all-to-all-done = bf16[512,8,128]{2,1,0:T(8,128)(2,1)S(1)} async-done(((bf16[512,8,128]{2,1,0:T(8,128)(2,1)}), bf16[512,8,128]{2,1,0:T(8,128)(2,1)S(1)}, u32[]{:S(2)}, u32[]{:S(2)}) %all-to-all-start) | async-done | bytes 1048608 | tf_op jit(solution)/shard_map/all_to_all | solution.py:235
  57.1 0.3 broadcast_in_dim.7.seen_any.seen_ref
  57.5 1.4 %pick_pages.1 = bf16[64,64,128]{2,1,0:T(8,128)(2,1)S(1)} custom-call(bf16[1024,1024]{1,0:T(8,128)(2,1)S(1)} %fusion.chosen_ref, bf16[256,16,128]{2,1,0:T(8,128)(2,1)S(1)} %bitcast.4, bf16[2048,128]{1,0:T(8,128)(2,1)S(1)} %broadcast_in_dim.7.seen_any.seen_ref), custom_call_target="tpu_custom_call" | custom-call | tf_op jit(solution)/shard_map/pick_pages/pallas_call | solution.py:126
  58.9 0.0 copy-start
  58.9 0.0 copy-start.1
  58.9 0.0 copy-start.2
  58.9 33.7 %all_to_all.10.held_ref = bf16[64,64,128]{2,1,0:T(8,128)(2,1)S(1)} all-to-all(bf16[64,64,128]{2,1,0:T(8,128)(2,1)S(1)} %pick_pages.1), channel_id=1, replica_groups=mesh['y_lo'=2,'x'=4,'z'=8,'y_hi'=4,'core'=2] {'y_lo','x','z'}, dimensions={0} | all-to-all | bytes 2097152 | tf_op jit(solution)/shard_map/all_to_all | solution.py:235
  92.7 0.0 copy-done
  92.7 0.0 copy-done.1
  92.7 0.0 copy-done.2
  92.7 3.5 %attend.1 = bf16[64,2048]{1,0:T(8,128)(2,1)} custom-call(bf16[64,2048]{1,0:T(8,128)(2,1)S(1)} %copy-done, bf16[64,128]{1,0:T(8,128)(2,1)S(1)} %copy-done.1, bf16[64,128]{1,0:T(8,128)(2,1)S(1)} %copy-done.2, bf16[64,64,128]{2,1,0:T(8,128)(2,1)S(1)} %all_to_all.10.held_ref, bf16[2048,128]{1,0:T(8,128)(2,1)S(1)} %broadcast_in_dim.7.seen_any.seen_ref), custom_call_target="tpu_custom_call" | custom-call | tf_op jit(solution)/shard_map/attend/pallas_call | solution.py:218
  (2 shorter events, 0.0 us)
Async XLA Ops:
  0.0 24.7 %copy-start.4 = (s32[64]{0:T(128)S(1)}, s32[64]{0:T(128)}, u32[]{:S(2)}) copy-start(s32[64]{0:T(128)} %param.13) | copy-start | bytes 772
  0.0 25.3 %copy-start.3 = (s32[64,16]{0,1:T(8,128)S(1)}, s32[64,16]{0,1:T(8,128)}, u32[]{:S(2)}) copy-start(s32[64,16]{0,1:T(8,128)} %param.12) | copy-start | bytes 12292
  2.5 54.6 %all-to-all-start = ((bf16[512,8,128]{2,1,0:T(8,128)(2,1)}), bf16[512,8,128]{2,1,0:T(8,128)(2,1)S(1)}, u32[]{:S(2)}, u32[]{:S(2)}) async-start(bf16[512,8,128]{2,1,0:T(8,128)(2,1)} %bitcast.5), calls=%async_computation | async-start | bytes 2097152 | tf_op jit(solution)/shard_map/all_to_all | solution.py:235
  58.9 33.8 %copy-start = (bf16[64,2048]{1,0:T(8,128)(2,1)S(1)}, bf16[64,2048]{1,0:T(8,128)(2,1)}, u32[]{:S(2)}) copy-start(bf16[64,2048]{1,0:T(8,128)(2,1)} %query_ref.1) | copy-start | bytes 786436
  58.9 33.8 %copy-start.1 = (bf16[64,128]{1,0:T(8,128)(2,1)S(1)}, bf16[64,128]{1,0:T(8,128)(2,1)}, u32[]{:S(2)}) copy-start(bf16[64,128]{1,0:T(8,128)(2,1)} %key_ref.1) | copy-start | bytes 49156
  58.9 33.8 %copy-start.2 = (bf16[64,128]{1,0:T(8,128)(2,1)S(1)}, bf16[64,128]{1,0:T(8,128)(2,1)}, u32[]{:S(2)}) copy-start(bf16[64,128]{1,0:T(8,128)(2,1)} %value_ref.1) | copy-start | bytes 49156
